TPU v7x, 128 devices: a whole 4x4x4 slice. The times are simulated.
128 devices in a mesh: shard: 8 (over x_lo, z), replica: 16 (over x_hi, y, core).
Axes of the slice: x: 4 (x_hi: 2, x_lo: 2; x = x_hi * 2 + x_lo), y: 4, z: 4, core: 2. Of those that a mesh axis runs over, the one named last changes fastest.
Arguments:
- tokens: bfloat16 [16, 1024, 1024], P('replica', 'shard'), may hold values from -6 to 6
- segment_ids: int32 [16, 1024], P('replica', 'shard'), may hold values from 0 to 3, as said below
- cotangent: bfloat16 [16, 1024, 1024], P('replica', 'shard'), may hold values from -6 to 6
- gain1: bfloat16 [2, 1024], P(None, 'shard'), may hold values from 0.5 to 1.5
- shift1: bfloat16 [2, 1024], P(None, 'shard'), may hold values from -1.5 to 1.5
- qkv_weight: bfloat16 [2, 1024, 3072], P(None, 'shard'), may hold values from -0.5 to 0.5
- qv_bias: bfloat16 [2, 2048], P(None, 'shard'), may hold values from -1.5 to 1.5
- out_weight: bfloat16 [2, 1024, 1024], P(None, 'shard'), may hold values from -0.75 to 0.75
- out_bias: bfloat16 [2, 1024], P(None, 'shard'), may hold values from -1.5 to 1.5
- gain2: bfloat16 [2, 1024], P(None, 'shard'), may hold values from 0.5 to 1.5
- shift2: bfloat16 [2, 1024], P(None, 'shard'), may hold values from -1.5 to 1.5
- up_weight: bfloat16 [2, 1024, 4096], P(None, 'shard'), may hold values from -0.1875 to 0.1875
- up_bias: bfloat16 [2, 4096], P(None, 'shard'), may hold values from -1.5 to 1.5
- down_weight: bfloat16 [2, 4096, 1024], P(None, 'shard'), may hold values from -0.09375 to 0.09375
- down_bias: bfloat16 [2, 1024], P(None, 'shard'), may hold values from -1.5 to 1.5
Outputs:
- output: bfloat16 [16, 1024, 1024], P('replica', 'shard')
- tokens_grad: float32 [16, 1024, 1024], P('replica', 'shard')
- gain1_grad: float32 [2, 1024], P(None, 'shard')
- shift1_grad: float32 [2, 1024], P(None, 'shard')
- qkv_weight_grad: float32 [2, 1024, 3072], P(None, 'shard')
- qv_bias_grad: float32 [2, 2048], P(None, 'shard')
- out_weight_grad: float32 [2, 1024, 1024], P(None, 'shard')
- out_bias_grad: float32 [2, 1024], P(None, 'shard')
- gain2_grad: float32 [2, 1024], P(None, 'shard')
- shift2_grad: float32 [2, 1024], P(None, 'shard')
- up_weight_grad: float32 [2, 1024, 4096], P(None, 'shard')
- up_bias_grad: float32 [2, 4096], P(None, 'shard')
- down_weight_grad: float32 [2, 4096, 1024], P(None, 'shard')
- down_bias_grad: float32 [2, 1024], P(None, 'shard')
Inputs may be any that keep to these rules, and one draw needn't show every extreme that they name: `segment_ids`: along each group's 1024 tokens the ids never fall and take the values 0, 1, 2, 3 (four packed documents of uneven lengths); document 1 begins among the group's first 128 tokens and ends among its last 128.
All inputs are finite; a program needn't handle non-finite values.
Results may differ from a plain program's by a relative error of at most 0.025.
Values may be sent and summed in bfloat16 or wider, within the bound.
A program may use at most 256 MiB of HBM per device.

v0:
```python
import math

import jax
import jax.numpy as jnp
from jax import lax
from jax.sharding import PartitionSpec as P

H = 16
HD = 64
LAYERS = 2


masked_value = -1e30


def normalize(rows, gain, shift):
    mean = jnp.mean(rows, axis=-1, keepdims=True)
    centered = rows - mean
    variance = jnp.mean(centered * centered, axis=-1, keepdims=True)
    return centered * lax.rsqrt(variance + 1e-05) * gain + shift


def smooth(values):
    return jax.nn.gelu(values, approximate=True)


def head_slopes():
    return 2.0 ** (-8.0 * (jnp.arange(H, dtype=jnp.float32) + 1.0) / H)


def score_block(query, keys, query_start, query_segs, key_segs):
    rows = query.shape[0]
    group = keys.shape[0]
    scores = jnp.einsum(
        "qhd,khd->hqk",
        query.reshape(rows, H, HD),
        keys.reshape(group, H, HD),
        preferred_element_type=jnp.float32,
    ) * (1.0 / math.sqrt(HD))
    query_pos = query_start + jnp.arange(rows, dtype=jnp.int32)
    key_pos = jnp.arange(group, dtype=jnp.int32)
    distance = (query_pos[:, None] - key_pos[None, :]).astype(jnp.float32)
    scores = scores - head_slopes()[:, None, None] * distance[None]
    allowed = (query_segs[:, None] == key_segs[None, :]) & (query_pos[:, None] >= key_pos[None, :])
    return jnp.where(allowed[None], scores, masked_value)


def forward_layer(state, gathered, own_segs, offset):
    gain_a, shift_a, w_qkv, b_qv, w_out, b_out, gain_b, shift_b, w_up, b_up, w_down, b_down = (
        gathered
    )
    rows = state.shape[0]
    width = w_out.shape[0]
    hidden_low = normalize(state, gain_a.astype(jnp.float32), shift_a.astype(jnp.float32)).astype(
        jnp.bfloat16
    )
    bias = jnp.concatenate(
        [
            b_qv[:width].astype(jnp.float32),
            jnp.zeros((width,), jnp.float32),
            b_qv[width:].astype(jnp.float32),
        ]
    )
    projected = (jnp.dot(hidden_low, w_qkv, preferred_element_type=jnp.float32) + bias).astype(
        jnp.bfloat16
    )
    query = projected[:, :width]
    keys, values, all_segs = (
        lax.all_gather(projected[:, width : 2 * width], "shard", axis=0, tiled=True),
        lax.all_gather(projected[:, 2 * width :], "shard", axis=0, tiled=True),
        lax.all_gather(own_segs, "shard", axis=0, tiled=True),
    )
    group = keys.shape[0]
    scores = score_block(query, keys, offset, own_segs, all_segs)
    top = jnp.max(scores, axis=-1, keepdims=True)
    expo = jnp.exp(scores - top)
    total = jnp.sum(expo, axis=-1, keepdims=True)
    probs = expo / total
    log_total = top + jnp.log(total)
    mixed = jnp.einsum(
        "hqk,khd->qhd",
        probs.astype(jnp.bfloat16),
        values.reshape(group, H, HD),
        preferred_element_type=jnp.float32,
    )
    mixed = mixed.reshape(rows, width).astype(jnp.bfloat16)
    middle = (
        state
        + jnp.dot(mixed, w_out, preferred_element_type=jnp.float32)
        + b_out.astype(jnp.float32)
    )
    hidden2_low = normalize(middle, gain_b.astype(jnp.float32), shift_b.astype(jnp.float32)).astype(
        jnp.bfloat16
    )
    upped = jnp.dot(hidden2_low, w_up, preferred_element_type=jnp.float32) + b_up.astype(
        jnp.float32
    )
    active = smooth(upped).astype(jnp.bfloat16)
    state_next = (
        middle
        + jnp.dot(active, w_down, preferred_element_type=jnp.float32)
        + b_down.astype(jnp.float32)
    )
    return (
        state_next,
        (
            state,
            hidden_low,
            query,
            keys,
            values,
            all_segs,
            log_total,
            mixed,
            middle,
            hidden2_low,
            upped,
            active,
        ),
    )


def column_sum(values):
    return jnp.sum(values.astype(jnp.float32), axis=0)


def backward_layer(grad, saved, gathered, own_segs, offset):
    gain_a, shift_a, w_qkv, b_qv, w_out, b_out, gain_b, shift_b, w_up, b_up, w_down, b_down = (
        gathered
    )
    (
        state_in,
        hidden_low,
        query,
        keys,
        values,
        all_segs,
        log_total,
        mixed,
        middle,
        hidden2_low,
        upped,
        active,
    ) = saved
    rows = state_in.shape[0]
    width = w_out.shape[0]
    group = keys.shape[0]
    d_down = grad.astype(jnp.bfloat16)
    g_down_bias = column_sum(d_down)
    g_down = jnp.einsum("rf,rd->fd", active, d_down, preferred_element_type=jnp.float32)
    d_active = jnp.einsum("rd,fd->rf", d_down, w_down, preferred_element_type=jnp.float32)
    gelu_back = jax.vjp(smooth, upped)[1]
    d_upped = gelu_back(d_active)[0].astype(jnp.bfloat16)
    g_up_bias = column_sum(d_upped)
    g_up = jnp.einsum("rd,rf->df", hidden2_low, d_upped, preferred_element_type=jnp.float32)
    d_hidden2 = jnp.einsum("rf,df->rd", d_upped, w_up, preferred_element_type=jnp.float32)
    norm_back = jax.vjp(normalize, middle, gain_b.astype(jnp.float32), shift_b.astype(jnp.float32))[
        1
    ]
    d_mid_norm, g_gain_b, g_shift_b = norm_back(d_hidden2)
    d_middle = grad + d_mid_norm
    d_branch = d_middle.astype(jnp.bfloat16)
    g_out_bias = column_sum(d_branch)
    g_out = jnp.einsum("re,rd->ed", mixed, d_branch, preferred_element_type=jnp.float32)
    d_mixed = jnp.einsum("rd,ed->re", d_branch, w_out, preferred_element_type=jnp.float32).astype(
        jnp.bfloat16
    )
    scores = score_block(query, keys, offset, own_segs, all_segs)
    probs = jnp.exp(scores - log_total)
    heads_mixed = d_mixed.reshape(rows, H, HD)
    d_probs = jnp.einsum(
        "qhd,khd->hqk",
        heads_mixed,
        values.reshape(group, H, HD),
        preferred_element_type=jnp.float32,
    )
    row_delta = jnp.sum(d_probs * probs, axis=-1, keepdims=True)
    d_scores = (probs * (d_probs - row_delta)).astype(jnp.bfloat16)
    factor = 1.0 / math.sqrt(HD)
    d_query = (
        (
            jnp.einsum(
                "hqk,khd->qhd",
                d_scores,
                keys.reshape(group, H, HD),
                preferred_element_type=jnp.float32,
            )
            * factor
        )
        .reshape(rows, width)
        .astype(jnp.bfloat16)
    )
    key_part = (
        jnp.einsum(
            "hqk,qhd->khd", d_scores, query.reshape(rows, H, HD), preferred_element_type=jnp.float32
        ).reshape(group, width)
        * factor
    )
    value_part = jnp.einsum(
        "hqk,qhd->khd", probs.astype(jnp.bfloat16), heads_mixed, preferred_element_type=jnp.float32
    ).reshape(group, width)
    d_key, d_value = (
        lax.psum_scatter(
            key_part.astype(jnp.bfloat16), "shard", scatter_dimension=0, tiled=True
        ).astype(jnp.float32),
        lax.psum_scatter(
            value_part.astype(jnp.bfloat16), "shard", scatter_dimension=0, tiled=True
        ).astype(jnp.float32),
    )
    d_key = d_key.astype(jnp.bfloat16)
    d_value = d_value.astype(jnp.bfloat16)
    d_projected = jnp.concatenate([d_query, d_key, d_value], axis=1)
    g_qkv = jnp.einsum("rd,rc->dc", hidden_low, d_projected, preferred_element_type=jnp.float32)
    g_qv_bias = jnp.concatenate([column_sum(d_query), column_sum(d_value)])
    d_hidden = jnp.einsum("rc,dc->rd", d_projected, w_qkv, preferred_element_type=jnp.float32)
    norm_back = jax.vjp(
        normalize, state_in, gain_a.astype(jnp.float32), shift_a.astype(jnp.float32)
    )[1]
    d_state, g_gain_a, g_shift_a = norm_back(d_hidden)
    return (
        d_middle + d_state,
        (
            g_gain_a,
            g_shift_a,
            g_qkv,
            g_qv_bias,
            g_out,
            g_out_bias,
            g_gain_b,
            g_shift_b,
            g_up,
            g_up_bias,
            g_down,
            g_down_bias,
        ),
    )


def share_grads(full):
    (
        g_gain_a,
        g_shift_a,
        g_qkv,
        g_qv_bias,
        g_out,
        g_out_bias,
        g_gain_b,
        g_shift_b,
        g_up,
        g_up_bias,
        g_down,
        g_down_bias,
    ) = full
    owned = (
        lax.psum_scatter(
            g_gain_a.astype(jnp.bfloat16), "shard", scatter_dimension=0, tiled=True
        ).astype(jnp.float32),
        lax.psum_scatter(
            g_shift_a.astype(jnp.bfloat16), "shard", scatter_dimension=0, tiled=True
        ).astype(jnp.float32),
        lax.psum_scatter(
            g_qkv.astype(jnp.bfloat16), "shard", scatter_dimension=0, tiled=True
        ).astype(jnp.float32),
        lax.psum_scatter(
            g_qv_bias.astype(jnp.bfloat16), "shard", scatter_dimension=0, tiled=True
        ).astype(jnp.float32),
        lax.psum_scatter(
            g_out.astype(jnp.bfloat16), "shard", scatter_dimension=0, tiled=True
        ).astype(jnp.float32),
        lax.psum_scatter(
            g_out_bias.astype(jnp.bfloat16), "shard", scatter_dimension=0, tiled=True
        ).astype(jnp.float32),
        lax.psum_scatter(
            g_gain_b.astype(jnp.bfloat16), "shard", scatter_dimension=0, tiled=True
        ).astype(jnp.float32),
        lax.psum_scatter(
            g_shift_b.astype(jnp.bfloat16), "shard", scatter_dimension=0, tiled=True
        ).astype(jnp.float32),
        lax.psum_scatter(
            g_up.astype(jnp.bfloat16), "shard", scatter_dimension=0, tiled=True
        ).astype(jnp.float32),
        lax.psum_scatter(
            g_up_bias.astype(jnp.bfloat16), "shard", scatter_dimension=0, tiled=True
        ).astype(jnp.float32),
        lax.psum_scatter(
            g_down.astype(jnp.bfloat16), "shard", scatter_dimension=0, tiled=True
        ).astype(jnp.float32),
        lax.psum_scatter(
            g_down_bias.astype(jnp.bfloat16), "shard", scatter_dimension=0, tiled=True
        ).astype(jnp.float32),
    )
    (
        o_gain_a,
        o_shift_a,
        o_qkv,
        o_qv_bias,
        o_out,
        o_out_bias,
        o_gain_b,
        o_shift_b,
        o_up,
        o_up_bias,
        o_down,
        o_down_bias,
    ) = owned
    return (
        lax.psum(o_gain_a.astype(jnp.bfloat16), "replica").astype(jnp.float32),
        lax.psum(o_shift_a.astype(jnp.bfloat16), "replica").astype(jnp.float32),
        lax.psum(o_qkv.astype(jnp.bfloat16), "replica").astype(jnp.float32),
        lax.psum(o_qv_bias.astype(jnp.bfloat16), "replica").astype(jnp.float32),
        lax.psum(o_out.astype(jnp.bfloat16), "replica").astype(jnp.float32),
        lax.psum(o_out_bias.astype(jnp.bfloat16), "replica").astype(jnp.float32),
        lax.psum(o_gain_b.astype(jnp.bfloat16), "replica").astype(jnp.float32),
        lax.psum(o_shift_b.astype(jnp.bfloat16), "replica").astype(jnp.float32),
        lax.psum(o_up.astype(jnp.bfloat16), "replica").astype(jnp.float32),
        lax.psum(o_up_bias.astype(jnp.bfloat16), "replica").astype(jnp.float32),
        lax.psum(o_down.astype(jnp.bfloat16), "replica").astype(jnp.float32),
        lax.psum(o_down_bias.astype(jnp.bfloat16), "replica").astype(jnp.float32),
    )


def per_device(
    tokens,
    segment_ids,
    cotangent,
    gain1,
    shift1,
    qkv_weight,
    qv_bias,
    out_weight,
    out_bias,
    gain2,
    shift2,
    up_weight,
    up_bias,
    down_weight,
    down_bias,
):
    rows = tokens.shape[1]
    offset = lax.axis_index("shard") * rows
    own_segs = segment_ids[0]
    state = tokens[0].astype(jnp.float32)
    saved_all = []
    gathered_all = []
    for index in range(LAYERS):
        gathered = (
            lax.all_gather(gain1[index], "shard", axis=0, tiled=True),
            lax.all_gather(shift1[index], "shard", axis=0, tiled=True),
            lax.all_gather(qkv_weight[index], "shard", axis=0, tiled=True),
            lax.all_gather(qv_bias[index], "shard", axis=0, tiled=True),
            lax.all_gather(out_weight[index], "shard", axis=0, tiled=True),
            lax.all_gather(out_bias[index], "shard", axis=0, tiled=True),
            lax.all_gather(gain2[index], "shard", axis=0, tiled=True),
            lax.all_gather(shift2[index], "shard", axis=0, tiled=True),
            lax.all_gather(up_weight[index], "shard", axis=0, tiled=True),
            lax.all_gather(up_bias[index], "shard", axis=0, tiled=True),
            lax.all_gather(down_weight[index], "shard", axis=0, tiled=True),
            lax.all_gather(down_bias[index], "shard", axis=0, tiled=True),
        )
        state, saved = forward_layer(state, gathered, own_segs, offset)
        saved_all.append(saved)
        gathered_all.append(gathered)
    output = state.astype(jnp.bfloat16)[None]
    grad = cotangent[0].astype(jnp.float32)
    results = []
    for index in reversed(range(LAYERS)):
        gathered = (
            lax.all_gather(gain1[index], "shard", axis=0, tiled=True),
            lax.all_gather(shift1[index], "shard", axis=0, tiled=True),
            lax.all_gather(qkv_weight[index], "shard", axis=0, tiled=True),
            lax.all_gather(qv_bias[index], "shard", axis=0, tiled=True),
            lax.all_gather(out_weight[index], "shard", axis=0, tiled=True),
            lax.all_gather(out_bias[index], "shard", axis=0, tiled=True),
            lax.all_gather(gain2[index], "shard", axis=0, tiled=True),
            lax.all_gather(shift2[index], "shard", axis=0, tiled=True),
            lax.all_gather(up_weight[index], "shard", axis=0, tiled=True),
            lax.all_gather(up_bias[index], "shard", axis=0, tiled=True),
            lax.all_gather(down_weight[index], "shard", axis=0, tiled=True),
            lax.all_gather(down_bias[index], "shard", axis=0, tiled=True),
        )
        grad, full = backward_layer(grad, saved_all[index], gathered, own_segs, offset)
        results.insert(0, share_grads(full))
    stacked = [
        jnp.stack([results[layer_index][member] for layer_index in range(LAYERS)])
        for member in range(12)
    ]
    return (
        output,
        grad[None],
        stacked[0],
        stacked[1],
        stacked[2],
        stacked[3],
        stacked[4],
        stacked[5],
        stacked[6],
        stacked[7],
        stacked[8],
        stacked[9],
        stacked[10],
        stacked[11],
    )


def solution(mesh):
    placed = (
        P("replica", "shard", None),
        P("replica", "shard"),
        P("replica", "shard", None),
        P(None, "shard"),
        P(None, "shard"),
        P(None, "shard", None),
        P(None, "shard"),
        P(None, "shard", None),
        P(None, "shard"),
        P(None, "shard"),
        P(None, "shard"),
        P(None, "shard", None),
        P(None, "shard"),
        P(None, "shard", None),
        P(None, "shard"),
    )
    return jax.shard_map(
        per_device,
        mesh=mesh,
        in_specs=placed,
        out_specs=(
            P("replica", "shard", None),
            P("replica", "shard", None),
            P(None, "shard"),
            P(None, "shard"),
            P(None, "shard", None),
            P(None, "shard"),
            P(None, "shard", None),
            P(None, "shard"),
            P(None, "shard"),
            P(None, "shard"),
            P(None, "shard", None),
            P(None, "shard"),
            P(None, "shard", None),
            P(None, "shard"),
        ),
        check_vma=False,
    )
```

profile of v0, /device:TPU:5, one launch (start us, length us, event | category | flops | bytes accessed | tf_op | source)
XLA Modules:
  0.0 1804.6 jit_solution(1032138021925362089)
XLA Ops:
  10.0 16.3 all-gather.1
  39.5 14.7 all-gather.16
  67.9 17.2 all-gather.46.cloned.1.call-done
  176.1 20.3 %all-gather.10 = bf16[1,4096]{1,0:T(2,128)(2,1)S(1)} all-gather(bf16[1,512]{1,0:T(2,128)(2,1)S(1)} %get-tuple-element.100), channel_id=12, replica_groups=mesh['shard'=8,'replica'=16] {'shard'}, dimensions={1}, use_global_device_ids=true | all-gather | bytes 9216 | tf_op jit(solution)/shard_map/all_gather | solution.py:356
  229.5 79.8 %all-gather.50.cloned.1.call-done = bf16[1,1024,4096]{2,1,0:T(8,128)(2,1)} async-done(((bf16[1,128,4096]{2,1,0:T(8,128)(2,1)}), bf16[1,1024,4096]{2,1,0:T(8,128)(2,1)}) %all-gather.50.cloned.1.call-update) | async-done | bytes 8388624 | tf_op jit(solution)/shard_map/all_gather | solution.py:355
  315.4 86.8 %all-gather.52.cloned.1.call-done = bf16[1,4096,1024]{2,1,0:T(8,128)(2,1)} async-done(((bf16[1,512,1024]{2,1,0:T(8,128)(2,1)}), bf16[1,4096,1024]{2,1,0:T(8,128)(2,1)}) %all-gather.52.cloned.1.call-update) | async-done | bytes 8388624 | tf_op jit(solution)/shard_map/all_gather | solution.py:357
  408.1 66.9 %all-gather.54.cloned.1.call-done = bf16[1,1024,3072]{2,1,0:T(8,128)(2,1)} async-done(((bf16[1,128,3072]{2,1,0:T(8,128)(2,1)}), bf16[1,1024,3072]{2,1,0:T(8,128)(2,1)}) %all-gather.54.cloned.1.call-update) | async-done | bytes 6291472 | tf_op jit(solution)/shard_map/all_gather | solution.py:349
  520.7 20.3 %all-gather.22 = bf16[1,4096]{1,0:T(2,128)(2,1)S(1)} all-gather(bf16[1,512]{1,0:T(2,128)(2,1)S(1)} %get-tuple-element.99), channel_id=24, replica_groups=mesh['shard'=8,'replica'=16] {'shard'}, dimensions={1}, use_global_device_ids=true | all-gather | bytes 9216 | tf_op jit(solution)/shard_map/all_gather | solution.py:356
  571.6 28.8 %all-gather.56.cloned.1.call-done = bf16[1,1024,1024]{2,1,0:T(8,128)(2,1)} async-done(((bf16[1,128,1024]{2,1,0:T(8,128)(2,1)}), bf16[1,1024,1024]{2,1,0:T(8,128)(2,1)}) %all-gather.56.cloned.1.call-update) | async-done | bytes 2097168 | tf_op jit(solution)/shard_map/all_gather | solution.py:351
  602.8 95.9 %all-gather.58.cloned.1.call-done = bf16[1,1024,4096]{2,1,0:T(8,128)(2,1)} async-done(((bf16[1,128,4096]{2,1,0:T(8,128)(2,1)}), bf16[1,1024,4096]{2,1,0:T(8,128)(2,1)}) %all-gather.58.cloned.1.call-update) | async-done | bytes 8388624 | tf_op jit(solution)/shard_map/all_gather | solution.py:355
  704.8 86.8 %all-gather.60.cloned.1.call-done = bf16[1,4096,1024]{2,1,0:T(8,128)(2,1)} async-done(((bf16[1,512,1024]{2,1,0:T(8,128)(2,1)}), bf16[1,4096,1024]{2,1,0:T(8,128)(2,1)}) %all-gather.60.cloned.1.call-update) | async-done | bytes 8388624 | tf_op jit(solution)/shard_map/all_gather | solution.py:357
  855.1 42.0 %reduce-scatter.37.cloned.1.call-done = bf16[128,1024]{1,0:T(8,128)(2,1)} async-done(((bf16[1024,1024]{1,0:T(8,128)(2,1)}), bf16[128,1024]{1,0:T(8,128)(2,1)}) %reduce-scatter.37.cloned.1.call-update) | async-done | bytes 262160
  979.5 35.3 %reduce-scatter.41.cloned.1.call-done = bf16[128,1024]{1,0:T(8,128)(2,1)} async-done(((bf16[1024,1024]{1,0:T(8,128)(2,1)}), bf16[128,1024]{1,0:T(8,128)(2,1)}) %reduce-scatter.41.cloned.1.call-update) | async-done | bytes 262160
  1036.9 22.2 %reduce-scatter.27.cloned.1.call-done = bf16[128,1024]{1,0:T(8,128)(2,1)} async-done(((bf16[1024,1024]{1,0:T(8,128)(2,1)}), bf16[128,1024]{1,0:T(8,128)(2,1)}) %reduce-scatter.27.cloned.1.call-update) | async-done | bytes 262160 | tf_op jit(solution)/shard_map/reduce_scatter | solution.py:267
  1059.1 43.5 %reduce-scatter.25.cloned.1.call-done = bf16[128,1024]{1,0:T(8,128)(2,1)} async-done(((bf16[1024,1024]{1,0:T(8,128)(2,1)}), bf16[128,1024]{1,0:T(8,128)(2,1)}) %reduce-scatter.25.cloned.1.call-update) | async-done | bytes 262160 | tf_op jit(solution)/shard_map/reduce_scatter | solution.py:267
  1102.6 79.4 %reduce-scatter.23.cloned.1.call-done = bf16[128,3072]{1,0:T(8,128)(2,1)} async-done(((bf16[1024,3072]{1,0:T(8,128)(2,1)}), bf16[128,3072]{1,0:T(8,128)(2,1)}) %reduce-scatter.23.cloned.1.call-update) | async-done | bytes 786448 | tf_op jit(solution)/shard_map/reduce_scatter | solution.py:261
  1182.0 93.8 %reduce-scatter.35.cloned.1.call-done = bf16[512,1024]{1,0:T(8,128)(2,1)} async-done(((bf16[4096,1024]{1,0:T(8,128)(2,1)}), bf16[512,1024]{1,0:T(8,128)(2,1)}) %reduce-scatter.35.cloned.1.call-update) | async-done | bytes 1048592 | tf_op jit(solution)/shard_map/reduce_scatter | solution.py:285
  1275.8 94.0 %reduce-scatter.31.cloned.1.call-done = bf16[128,4096]{1,0:T(8,128)(2,1)} async-done(((bf16[1024,4096]{1,0:T(8,128)(2,1)}), bf16[128,4096]{1,0:T(8,128)(2,1)}) %reduce-scatter.31.cloned.1.call-update) | async-done | bytes 1048592 | tf_op jit(solution)/shard_map/reduce_scatter | solution.py:279
  1369.8 74.2 %reduce-scatter.21.cloned.1.call-done = bf16[128,3072]{1,0:T(8,128)(2,1)} async-done(((bf16[1024,3072]{1,0:T(8,128)(2,1)}), bf16[128,3072]{1,0:T(8,128)(2,1)}) %reduce-scatter.21.cloned.1.call-update) | async-done | bytes 786448 | tf_op jit(solution)/shard_map/reduce_scatter | solution.py:261
  1444.0 94.0 %reduce-scatter.33.cloned.1.call-done = bf16[512,1024]{1,0:T(8,128)(2,1)} async-done(((bf16[4096,1024]{1,0:T(8,128)(2,1)}), bf16[512,1024]{1,0:T(8,128)(2,1)}) %reduce-scatter.33.cloned.1.call-update) | async-done | bytes 1048592 | tf_op jit(solution)/shard_map/reduce_scatter | solution.py:285
  1538.0 93.8 %reduce-scatter.29.cloned.1.call-done = bf16[128,4096]{1,0:T(8,128)(2,1)} async-done(((bf16[1024,4096]{1,0:T(8,128)(2,1)}), bf16[128,4096]{1,0:T(8,128)(2,1)}) %reduce-scatter.29.cloned.1.call-update) | async-done | bytes 1048592 | tf_op jit(solution)/shard_map/reduce_scatter | solution.py:279
  1659.8 27.1 %all-reduce.18 = (bf16[1024]{0:T(1024)(128)(2,1)S(1)}, bf16[1024]{0:T(1024)(128)(2,1)S(1)}, bf16[1024]{0:T(1024)(128)(2,1)S(1)}, bf16[1024]{0:T(1024)(128)(2,1)S...) all-reduce(bf16[1024]{0:T(1024)(128)(2,1)S(1)} %get-tuple-element.1, ...), channel_id=32, replica_groups=mesh['shard'=8,'replica'=16] {'shard'}, use_global_device_ids=true, to_apply=%region_30.31.clone | all-reduce | flops 24576 | bytes 98304
  1687.7 68.6 %all-reduce.16 = (bf16[1,128]{1,0:T(2,128)(2,1)S(1)}, bf16[1,128]{1,0:T(2,128)(2,1)S(1)}, bf16[1,128]{1,0:T(2,128)(2,1)S(1)}, bf16[1,128]{1,0:T(2,128)(2,1)S(1)}...) all-reduce(bf16[1,128]{1,0:T(2,128)(2,1)S(1)} %get-tuple-element.15, ...), channel_id=1, replica_groups=mesh['shard'=8,'replica'=16] {'replica'}, use_global_device_ids=true, to_apply=%region_31.32 | all-reduce | flops 3072 | bytes 12288 | tf_op jit(solution)/shard_map/psum | solution.py:307
  1761.9 26.5 %all-reduce.21.cloned.1.call-done = (bf16[1,128,3072]{2,1,0:T(8,128)(2,1)}, bf16[1,128,3072]{2,1,0:T(8,128)(2,1)}, bf16[1,128,1024]{2,1,0:T(8,128)(2,1)}, bf16[1...) async-done(((bf16[1,128,3072]{2,1,0:T(8,128)(2,1)}, ...) | async-done | bytes 6291472 | tf_op jit(solution)/shard_map/psum | solution.py:309
  (372 shorter events, 459.1 us)
Async XLA Ops:
  9.9 201.1 %all-gather.40.cloned.1.call-start = ((), (), s32[]{:S(2)}) async-start(), calls=%async_computation.13 | async-start | bytes 2359296 | tf_op jit(solution)/shard_map/all_gather | solution.py:69
  89.9 124.1 %all-gather.38.cloned.1.call-start = ((), (), s32[]{:S(2)}) async-start(), calls=%async_computation.12 | async-start | bytes 2359296 | tf_op jit(solution)/shard_map/all_gather | solution.py:70
  90.6 136.4 %all-gather.48.cloned.1.call-start = ((), (), s32[]{:S(2)}) async-start(), calls=%async_computation.25 | async-start | bytes 2359296 | tf_op jit(solution)/shard_map/all_gather | solution.py:351
  91.5 217.8 %all-gather.50.cloned.1.call-start = ((), (), s32[]{:S(2)}) async-start(), calls=%async_computation.26 | async-start | bytes 9437184 | tf_op jit(solution)/shard_map/all_gather | solution.py:355
  93.2 309.0 %all-gather.52.cloned.1.call-start = ((), (), s32[]{:S(2)}) async-start(), calls=%async_computation.27 | async-start | bytes 9437184 | tf_op jit(solution)/shard_map/all_gather | solution.py:357
  96.3 378.7 %all-gather.54.cloned.1.call-start = ((), (), s32[]{:S(2)}) async-start(), calls=%async_computation.28 | async-start | bytes 7077888 | tf_op jit(solution)/shard_map/all_gather | solution.py:349
  97.0 444.3 %all-gather.44.cloned.1.call-start = ((), (), s32[]{:S(2)}) async-start(), calls=%async_computation.15 | async-start | bytes 2359296 | tf_op jit(solution)/shard_map/all_gather | solution.py:69
  479.7 78.1 %all-gather.42.cloned.1.call-start = ((), (), s32[]{:S(2)}) async-start(), calls=%async_computation.14 | async-start | bytes 2359296 | tf_op jit(solution)/shard_map/all_gather | solution.py:70
  480.4 120.0 %all-gather.56.cloned.1.call-start = ((), (), s32[]{:S(2)}) async-start(), calls=%async_computation.29 | async-start | bytes 2359296 | tf_op jit(solution)/shard_map/all_gather | solution.py:351
  481.0 217.7 %all-gather.58.cloned.1.call-start = ((), (), s32[]{:S(2)}) async-start(), calls=%async_computation.30 | async-start | bytes 9437184 | tf_op jit(solution)/shard_map/all_gather | solution.py:355
  481.7 309.8 %all-gather.60.cloned.1.call-start = ((), (), s32[]{:S(2)}) async-start(), calls=%async_computation.31 | async-start | bytes 9437184 | tf_op jit(solution)/shard_map/all_gather | solution.py:357
  482.3 371.0 %reduce-scatter.39.cloned.1.call-start = ((), (), s32[]{:S(2)}) async-start(), calls=%async_computation.33 | async-start | bytes 2359296
  817.0 80.1 %reduce-scatter.37.cloned.1.call-start = ((), (), s32[]{:S(2)}) async-start(), calls=%async_computation.32 | async-start | bytes 2359296
  835.0 143.4 %reduce-scatter.43.cloned.1.call-start = ((), (), s32[]{:S(2)}) async-start(), calls=%async_computation.35 | async-start | bytes 2359296
  929.5 85.3 %reduce-scatter.41.cloned.1.call-start = ((), (), s32[]{:S(2)}) async-start(), calls=%async_computation.34 | async-start | bytes 2359296
  947.3 111.8 %reduce-scatter.27.cloned.1.call-start = ((), (), s32[]{:S(2)}) async-start(), calls=%async_computation.19 | async-start | bytes 2359296 | tf_op jit(solution)/shard_map/reduce_scatter | solution.py:267
  949.4 153.2 %reduce-scatter.25.cloned.1.call-start = ((), (), s32[]{:S(2)}) async-start(), calls=%async_computation.18 | async-start | bytes 2359296 | tf_op jit(solution)/shard_map/reduce_scatter | solution.py:267
  952.5 229.5 %reduce-scatter.23.cloned.1.call-start = ((), (), s32[]{:S(2)}) async-start(), calls=%async_computation.17 | async-start | bytes 7077888 | tf_op jit(solution)/shard_map/reduce_scatter | solution.py:261
  957.2 318.6 %reduce-scatter.35.cloned.1.call-start = ((), (), s32[]{:S(2)}) async-start(), calls=%async_computation.23 | async-start | bytes 9437184 | tf_op jit(solution)/shard_map/reduce_scatter | solution.py:285
  965.4 404.4 %reduce-scatter.31.cloned.1.call-start = ((), (), s32[]{:S(2)}) async-start(), calls=%async_computation.21 | async-start | bytes 9437184 | tf_op jit(solution)/shard_map/reduce_scatter | solution.py:279
  972.4 471.6 %reduce-scatter.21.cloned.1.call-start = ((), (), s32[]{:S(2)}) async-start(), calls=%async_computation.16 | async-start | bytes 7077888 | tf_op jit(solution)/shard_map/reduce_scatter | solution.py:261
  1021.6 516.4 %reduce-scatter.33.cloned.1.call-start = ((), (), s32[]{:S(2)}) async-start(), calls=%async_computation.22 | async-start | bytes 9437184 | tf_op jit(solution)/shard_map/reduce_scatter | solution.py:285
  1029.8 602.0 %reduce-scatter.29.cloned.1.call-start = ((), (), s32[]{:S(2)}) async-start(), calls=%async_computation.20 | async-start | bytes 9437184 | tf_op jit(solution)/shard_map/reduce_scatter | solution.py:279
  1036.8 751.6 %all-reduce.21.cloned.1.call-start = ((), (), s32[]{:S(2)}) async-start(), calls=%async_computation.36 | async-start | bytes 12582912 | tf_op jit(solution)/shard_map/psum | solution.py:309
  (73 other events, 1604.3 us)
Sparse Core Ops, SparseCore 0:
  10.3 74.7 all-gather.45
  127.2 40.6 all-gather.37
  169.4 40.9 all-gather.47
  212.5 96.8 all-gather.49
  311.4 90.7 all-gather.51
  403.8 71.0 all-gather.53
  479.8 35.1 all-gather.43
  517.2 40.5 all-gather.41
  559.3 41.0 all-gather.55
  602.1 96.5 all-gather.57
  700.7 90.7 all-gather.59
  817.1 36.1 reduce-scatter.38
  855.6 41.4 reduce-scatter.36
  929.6 41.4 reduce-scatter.42
  973.3 41.4 reduce-scatter.40
  1017.6 41.4 reduce-scatter.26
  1061.3 41.1 reduce-scatter.24
  1105.0 76.9 reduce-scatter.22
  1184.2 91.5 reduce-scatter.34
  1278.2 91.5 reduce-scatter.30
  1372.2 71.7 reduce-scatter.20
  1446.4 91.5 reduce-scatter.32
  1540.2 91.5 reduce-scatter.28
  1634.9 153.4 all-reduce.20
  (1 shorter events, 34.9 us)
where the time goes:
time: 1810 us; the launch traced here: 1800 us
  waiting for transfers between devices  1190 us (66%)
  blocking collectives  336 us (19%)
  matrix products  161 us (9%)
  local copies, waits for them, and re-layouts  66 us (4%)
  other arithmetic  31.3 us (2%)
    reduce_scatter x2, waiting for transfers between devices, share_grads(): lax.psum_scatter(g_down.astype(jnp.bfloat16), 'shard', scatter_dimension=...  188 us
    reduce_scatter x2, waiting for transfers between devices, share_grads(): lax.psum_scatter(g_up.astype(jnp.bfloat16), 'shard', scatter_dimension=0,...  188 us
    all_gather x2, waiting for transfers between devices, per_device(): lax.all_gather(up_weight[index], 'shard', axis=0, tiled=True)  176 us
    all_gather x2, waiting for transfers between devices, per_device(): lax.all_gather(down_weight[index], 'shard', axis=0, tiled=True)  174 us
    reduce_scatter x2, waiting for transfers between devices, share_grads(): lax.psum_scatter(g_qkv.astype(jnp.bfloat16), 'shard', scatter_dimension=0...  154 us
    unnamed x29, waiting for transfers between devices  95.2 us
    all_gather x2, waiting for transfers between devices, per_device(): lax.all_gather(qkv_weight[index], 'shard', axis=0, tiled=True)  84.1 us
    psum x1, blocking collectives, share_grads(): lax.psum(o_gain_a.astype(jnp.bfloat16), 'replica').astype(jnp.float32)  68.6 us
  transfers between devices with their start and end apart: 25, of which 20 were waited for; matrix products, arithmetic and copies ran while one was open for 9% of the time, Pallas kernels for 0%

commit v1 on v0

v1 whole, which is shorter than its diff:
```python
import functools
import math

import jax
import jax.numpy as jnp
from jax import lax
from jax.experimental import pallas as pl
from jax.experimental.pallas import tpu as pltpu
from jax.sharding import PartitionSpec as P

D = 1024
H = 16
HD = 64
FF = 4096
LAYERS = 2
GROUP = 1024
OWN = 128
N = 8
WQ = 3 * D // N
WU = FF // N
WA = WQ + WU
QB = 256
KC = 128
MASKED = -1e30
EPS = 1e-5
MESH = pl.DeviceIdType.MESH
F32 = jnp.float32
BF16 = jnp.bfloat16
VMEM_LIMIT = 60 * 1024 * 1024

NN = (((1,), (0,)), ((), ()))
NT = (((1,), (1,)), ((), ()))
TN = (((0,), (0,)), ((), ()))


def dot(left, right, dims=NN):
    return lax.dot_general(left, right, dims, preferred_element_type=F32)


class Place:
    def __init__(self, y_size):
        self.shard = lax.axis_index("shard")
        self.replica = lax.axis_index("replica")
        self.side, self.z = self.shard // 4, self.shard % 4
        self.chip, self.core = self.replica // 2, self.replica % 2
        self.y_size = y_size
        self.y = self.chip % y_size
        self.block = self.core * 4 + self.z
        right, left, far = (self.z + 1) % 4, (self.z + 3) % 4, (self.z + 2) % 4
        self.right = {"shard": self.side * 4 + right}
        self.left = {"shard": self.side * 4 + left}
        self.twin = {"replica": self.chip * 2 + 1 - self.core}
        mine, other = self.core * 4, (1 - self.core) * 4
        self.right_block, self.left_block, self.far_block = mine + right, mine + left, mine + far
        self.twin_block = other + self.z
        self.twin_right, self.twin_left, self.twin_far = other + right, other + left, other + far
        opposite = (1 - self.side) * 4 + self.z
        self.partner = {"shard": opposite, "replica": self.chip * 2 + 1 - self.core}
        self.needs_x = {"shard": opposite, "replica": self.chip * 2 + self.side}
        self.moves = self.core != self.side

    def at_shard(self, j):
        return {"shard": (self.shard + j) % N}

    def at_block(self, flip, j):
        core = self.core if flip == 0 else 1 - self.core
        return {"shard": (self.shard + j) % N, "replica": self.chip * 2 + core}

    def at_y(self, j):
        chip = self.chip - self.y + (self.y + j) % self.y_size
        return {"replica": chip * 2 + self.core}

    def greet(self, replicas):
        barrier = pltpu.get_barrier_semaphore()
        for i in range(N):
            for j in range(replicas):
                if i + j > 0:
                    peer = {"shard": (self.shard + i) % N, "replica": (self.replica + j) % replicas}
                    pl.semaphore_signal(barrier, inc=1, device_id=peer, device_id_type=MESH)
        pl.semaphore_wait(barrier, N * replicas - 1)


def block(index, rows=OWN, start=0):
    return pl.ds(pl.multiple_of(index * OWN + start, 16), rows)


def lanes_of(index):
    return pl.ds(pl.multiple_of(index * OWN, OWN), OWN)


class Links:
    def __init__(self, send_sems, recv_sems):
        self.send_sems, self.recv_sems, self.used = send_sems, recv_sems, 0

    def pair(self, count=1):
        index = self.used
        self.used += count
        return index

    def make(self, src, dst, peer, send, recv):
        return pltpu.make_async_remote_copy(
            src_ref=src,
            dst_ref=dst,
            send_sem=self.send_sems.at[send],
            recv_sem=self.recv_sems.at[recv],
            device_id=peer,
            device_id_type=MESH,
        )

    def copy(self, src, dst, peer):
        index = self.pair()
        copy = self.make(src, dst, peer, index, index)
        copy.start()
        return copy

    def local(self, src, dst, recv):
        pltpu.make_async_copy(src, dst, self.recv_sems.at[recv]).start()

    def landed(self, ref, recv):
        pltpu.make_async_copy(ref, ref, self.recv_sems.at[recv]).wait()

    def sent(self, ref, send):
        pltpu.make_async_copy(ref, ref, self.send_sems.at[send]).wait()


def gather(links, place, full, use):
    p = place
    half = OWN // 2

    def send(index, peer, rows=OWN, start=0):
        ref = full.at[block(index, rows, start), :]
        return links.copy(ref, ref, peer)

    low_r = send(p.block, p.right, half, 0)
    high_l = send(p.block, p.left, half, half)
    own_t = send(p.block, p.twin)
    high_r = send(p.block, p.right, half, half)
    low_l = send(p.block, p.left, half, 0)
    use(p.block)
    own_t.wait_recv()
    use(p.twin_block)
    low_r.wait_recv()
    far_low = send(p.left_block, p.right, half, 0)
    high_l.wait_recv()
    far_high = send(p.right_block, p.left, half, half)
    high_r.wait_recv()
    left_t = send(p.left_block, p.twin)
    low_l.wait_recv()
    right_t = send(p.right_block, p.twin)
    use(p.left_block)
    use(p.right_block)
    left_t.wait_recv()
    use(p.twin_left)
    right_t.wait_recv()
    use(p.twin_right)
    far_low.wait_recv()
    low_t = send(p.far_block, p.twin, half, 0)
    far_high.wait_recv()
    high_t = send(p.far_block, p.twin, half, half)
    use(p.far_block)
    low_t.wait_recv()
    high_t.wait_recv()
    use(p.twin_far)
    for copy in (low_r, high_l, own_t, high_r, low_l, far_low, far_high, left_t, right_t, low_t, high_t):
        copy.wait_send()


GATHER_COPIES = 11


def scatter(links, place, make, out, slots, beside=()):
    p = place
    half = OWN // 2
    beside = list(beside) + [lambda: None] * 2

    def rows_of(role, rows=OWN, start=0):
        return pl.ds(role * OWN + start, rows)

    def send(role, slot, peer, rows=OWN, start=0):
        return links.copy(out.at[rows_of(role, rows, start), :], slots.at[rows_of(slot, rows, start), :], peer)

    def fill(role, index):
        out[rows_of(role), :] = make(index).astype(BF16)

    def add(role, slot, rows=OWN, start=0):
        mine, theirs = rows_of(role, rows, start), rows_of(slot, rows, start)
        out[mine, :] = (out[mine, :].astype(F32) + slots[theirs, :].astype(F32)).astype(BF16)

    twins = []
    for role, index in enumerate((p.twin_far, p.twin_right, p.twin_left, p.twin_block)):
        fill(role, index)
        twins.append(send(role, role, p.twin))
    fill(4, p.far_block)
    twins[0].wait_recv()
    add(4, 0)
    far_low = send(4, 4, p.right, half, 0)
    far_high = send(4, 4, p.left, half, half)
    fill(5, p.right_block)
    twins[1].wait_recv()
    add(5, 1)
    high_r = send(5, 5, p.right, half, half)
    fill(6, p.left_block)
    twins[2].wait_recv()
    add(6, 2)
    low_l = send(6, 6, p.left, half, 0)
    own = make(p.block)
    twins[3].wait_recv()
    own = own + slots[rows_of(3), :].astype(F32)
    beside[0]()
    far_low.wait_recv()
    add(5, 4, half, 0)
    low_r = send(5, 5, p.right, half, 0)
    far_high.wait_recv()
    add(6, 4, half, half)
    high_l = send(6, 6, p.left, half, half)
    beside[1]()
    for copy in (high_r, low_l, low_r, high_l):
        copy.wait_recv()
    own = own + slots[rows_of(5), :].astype(F32) + slots[rows_of(6), :].astype(F32)
    for copy in twins + [far_low, far_high, high_r, low_l, low_r, high_l]:
        copy.wait_send()
    return own


SCATTER_COPIES = 10


def standardize(rows):
    mean = jnp.mean(rows, axis=-1, keepdims=True)
    centered = rows - mean
    variance = jnp.mean(centered * centered, axis=-1, keepdims=True)
    scale = lax.rsqrt(variance + EPS)
    return centered * scale, scale


def normalize_back(rows, gain, grad):
    unit, scale = standardize(rows)
    d_unit = grad * gain
    mean = jnp.mean(d_unit, axis=-1, keepdims=True)
    along = jnp.mean(d_unit * unit, axis=-1, keepdims=True)
    d_rows = scale * (d_unit - mean - unit * along)
    d_gain = jnp.sum(grad * unit, axis=0, keepdims=True)
    d_shift = jnp.sum(grad, axis=0, keepdims=True)
    return d_rows, d_gain, d_shift


def gelu_pair(u):
    c = math.sqrt(2.0 / math.pi)
    square = u * u
    t = jnp.tanh(c * (u + 0.044715 * u * square))
    value = 0.5 * u * (1.0 + t)
    slope = 0.5 * (1.0 + t) + 0.5 * u * (1.0 - t * t) * (c * (1.0 + 3.0 * 0.044715 * square))
    return value, slope


def head_lanes(rows, head):
    lane = lax.broadcasted_iota(jnp.int32, (1, 2 * HD), 1)
    keep = (lane // HD) == head
    return jnp.where(keep, rows, jnp.zeros_like(rows))


def masked_scores(keys, query, slope, start, chunk, block_start, edge):
    scores = dot(keys, query, NT)
    row = lax.broadcasted_iota(jnp.int32, scores.shape, 0) + chunk
    scores = scores + slope * (row - block_start).astype(F32)
    keep = row >= start
    if edge:
        col = lax.broadcasted_iota(jnp.int32, scores.shape, 1) + block_start
        keep = keep & (row <= col)
    return jnp.where(keep, scores, MASKED)


class Weights:
    def __init__(self, links, place, raw, full):
        self.links, self.p = links, place
        self.raw, self.full = raw, full
        self.rows = OWN // place.y_size
        self.first = links.pair(4)
        self.second = links.pair(4)
        self.x = links.pair(4)

    def pieces(self, kind, l, peer_shard):
        p = self.p
        rows = pl.ds(pl.multiple_of(p.y * self.rows, 16), self.rows)
        take = p.core * 4 + peer_shard % 4
        dst = self.full[kind].at[l, p.shard, p.y]
        if kind == 0:
            for part in range(3):
                cols = pl.ds(pl.multiple_of(part * D + take * OWN, OWN), OWN)
                yield self.raw[0].at[l, rows, cols], dst.at[:, part * OWN : (part + 1) * OWN]
        else:
            yield self.raw[1].at[l, rows, pl.ds(pl.multiple_of(take * WU, OWN), WU)], dst

    def start(self, kind, l):
        sem = self.first + l * 2 + kind
        for j in range(1, N):
            peer = (self.p.shard + j) % N
            for src, dst in self.pieces(kind, l, peer):
                self.links.make(src, dst, {"shard": peer}, sem, sem).start()
        for src, dst in self.pieces(kind, l, self.p.shard):
            self.links.local(src, dst, sem)

    def around(self, kind, l):
        full = self.full[kind].at[l]
        self.links.landed(full.at[:, 0], self.first + l * 2 + kind)
        sem = self.second + l * 2 + kind
        for j in range(1, self.p.y_size):
            self.links.make(full.at[:, self.p.y], full.at[:, self.p.y], self.p.at_y(j), sem, sem).start()

    def ready(self, kind, l):
        if self.p.y_size > 1:
            self.links.landed(self.full[kind].at[l, :, 0 : self.p.y_size - 1], self.second + l * 2 + kind)

    def start_x(self):
        p = self.p
        for k in (2, 3):
            sem = self.x + (k - 2) * 2
            self.links.make(self.raw[k].at[p.core], self.full[k].at[p.core], p.needs_x, sem, sem + p.core).start()

        @pl.when(jnp.logical_not(p.moves))
        def _():
            for k in (2, 3):
                for l in range(LAYERS):
                    self.links.local(self.raw[k].at[l], self.full[k].at[l], self.x + (k - 2) * 2 + l)

    def ready_x(self, kind, l):
        self.links.landed(self.full[kind].at[l], self.x + (kind - 2) * 2 + l)

    def finish(self):
        for l in range(LAYERS):
            for kind in (0, 1):
                full = self.full[kind].at[l]
                self.links.sent(full.at[0 : N - 1, 0], self.first + l * 2 + kind)
                if self.p.y_size > 1:
                    self.links.sent(full.at[:, 0 : self.p.y_size - 1], self.second + l * 2 + kind)
        for k in (2, 3):
            self.links.sent(self.full[k].at[0], self.x + (k - 2) * 2)


class Swap:
    def __init__(self, links, place, src, dst):
        self.links, self.p, self.dst = links, place, dst
        self.sem = links.pair()
        self.copy = links.make(src, dst, place.partner, self.sem, self.sem)

        @pl.when(place.moves)
        def _():
            self.copy.start()

        @pl.when(jnp.logical_not(place.moves))
        def _():
            links.local(src, dst, self.sem)

    def ready(self):
        self.links.landed(self.dst, self.sem)

    def finish(self):
        @pl.when(self.p.moves)
        def _():
            self.copy.wait_send()


REPLICAS = 16
PLANE = 16
CHIPS = 8
HALF = OWN // 2
KINDS = ("up", "down", "qkv", "out")


class Sums:
    def __init__(self, links, place, l, wide, tall, slots, totals, outs):
        self.links, self.p, self.l = links, place, l
        self.wide, self.tall = wide, tall
        self.slots, self.totals, self.outs = slots, totals, outs
        self.q = place.side * 8 + place.chip
        self.sems = links.pair(len(KINDS))
        self.give = links.pair(len(KINDS))
        self.twin = links.pair(len(KINDS))
        self.last = {}

    def part(self, kind, q):
        if kind == "up":
            return self.wide.at[self.l, block_of(q, HALF), WQ:WA]
        if kind == "qkv":
            return self.wide.at[self.l, block_of(q, HALF), 0:WQ]
        rows = WU // 8 if kind == "down" else OWN // 8
        first = OWN if kind == "down" else 0
        return self.tall.at[self.l, pl.ds(pl.multiple_of(first + (q // 2) * rows, 16), rows), half_of(q % 2)]

    def target(self, kind):
        out = self.outs[kind]
        if kind in ("up", "qkv"):
            return out.at[self.l, self.p.block, self.q % 2]
        rows = WU // 8 if kind == "down" else OWN // 8
        return out.at[self.l, block_of(self.q // 2, rows), half_of(self.q % 2)]

    def region(self, kind, core):
        out = self.outs[kind]
        return out.at[self.l, pl.ds(core * 4, 4)] if kind in ("up", "qkv") else out.at[self.l, :, half_of(core)]

    def start(self, *kinds):
        for kind in kinds:
            sem = self.sems + KINDS.index(kind)
            for j in range(1, PLANE):
                q = (self.q + j) % PLANE
                peer = {"shard": (q // 8) * 4 + self.p.z, "replica": (q % 8) * 2 + self.p.core}
                self.links.make(self.part(kind, q), self.slots[kind].at[j - 1], peer, sem, sem).start()

    def total(self, *kinds):
        for kind in kinds:
            slots = self.slots[kind]
            self.links.landed(slots, self.sems + KINDS.index(kind))
            part = self.part(kind, self.q)[...].astype(F32)
            for j in range(PLANE - 1):
                part = part + slots[j].astype(F32)
            self.totals[kind][...] = part.astype(BF16)
            sem = self.give + KINDS.index(kind)
            by_rows = kind in ("up", "qkv")
            shard = self.q // 2 if by_rows else self.p.block
            core = self.p.core if by_rows else self.q % 2
            target = self.target(kind)
            for j in range(1, CHIPS):
                peer = {"shard": shard, "replica": ((self.p.chip + j) % CHIPS) * 2 + core}
                self.links.make(self.totals[kind], target, peer, sem, sem).start()
            mine = (shard == self.p.shard) & (core == self.p.core)
            last = self.links.make(self.totals[kind], target, {"shard": shard, "replica": self.p.chip * 2 + core}, sem, sem)
            pl.when(mine)(functools.partial(self.links.local, self.totals[kind], target, sem))
            pl.when(jnp.logical_not(mine))(last.start)
            self.last[kind] = (mine, last)

    def share(self, *kinds):
        for kind in kinds:
            region = self.region(kind, self.p.core)
            self.links.landed(region, self.give + KINDS.index(kind))
            self.links.make(region, region, self.p.twin, self.twin + KINDS.index(kind), self.twin + KINDS.index(kind)).start()

    def finish(self):
        for kind in KINDS:
            index = KINDS.index(kind)
            region = self.region(kind, self.p.core)
            self.links.landed(region, self.twin + index)
            self.links.sent(region, self.twin + index)
            self.links.sent(self.slots[kind], self.sems + index)
            self.links.sent(self.slots[kind].at[0 : CHIPS - 1], self.give + index)
            mine, last = self.last[kind]
            pl.when(jnp.logical_not(mine))(last.wait_send)


def block_of(index, rows):
    return pl.ds(pl.multiple_of(index * rows, 16), rows)


def half_of(index):
    return pl.ds(pl.multiple_of(index * (D // 2), OWN), D // 2)


def part_shapes():
    return {"up": (HALF, WU), "down": (WU // 8, D // 2), "qkv": (HALF, WQ), "out": (OWN // 8, D // 2)}


class SmallSums:
    def __init__(self, links, place, mine, low, slots, total, everyone, out):
        self.links, self.p = links, place
        self.mine, self.low, self.slots, self.sum, self.everyone, self.out = mine, low, slots, total, everyone, out
        self.first, self.second = links.pair(), links.pair()

    def start(self):
        self.low[...] = self.mine[...].astype(BF16)
        for j in range(1, N):
            peer = self.p.at_shard(j)
            src = self.low.at[:, lanes_of(peer["shard"])]
            self.links.make(src, self.slots.at[j - 1], peer, self.first, self.first).start()

    def total(self):
        self.links.landed(self.slots, self.first)
        total = self.mine[:, lanes_of(self.p.shard)]
        for j in range(N - 1):
            total = total + self.slots[j].astype(F32)
        self.sum[...] = total.astype(BF16)
        for j in range(1, REPLICAS):
            peer = {"replica": (self.p.replica + j) % REPLICAS}
            self.links.make(self.sum, self.everyone.at[j - 1], peer, self.second, self.second).start()

    def finish(self):
        self.links.landed(self.everyone, self.second)
        total = self.sum[...].astype(F32)
        for j in range(REPLICAS - 1):
            total = total + self.everyone[j].astype(F32)
        self.out[...] = total
        self.links.sent(self.slots, self.first)
        self.links.sent(self.everyone, self.second)


def blocks_kernel(
    y_size,
    tokens, cotangent, raw_qkv, raw_up, raw_out, raw_down, gain1, shift1, out_bias, gain2, shift2, down_bias,
    qv_bias, up_bias, own_ids,
    output, tokens_grad, up_out, down_out, qkv_out, out_out, small_out,
    wide, tall, mine, up_slots, down_slots, qkv_slots, out_slots, up_sum, down_sum, qkv_sum, out_sum,
    small_low, small_slots, small_sum, small_every,
    w_qkv, w_up, w_out, w_down, small_wide, small, segs, small_all, segs_all, vectors, ids, starts, slopes,
    token_in, cot_in, state, hidden1, qkv, lse, mixed, middle, hidden2, act_slope, active,
    score_scr, dprob_scr, turned, mixed_turned, d_full, d_upped, branch, d_mixed, d_qkv, dk_acc, dv_acc,
    out_scr, slots, low_out, grad, send_sems, recv_sems,
):
    place = Place(y_size)
    links = Links(send_sems, recv_sems)
    own = block(place.block)
    lanes = lanes_of(place.block)
    factor = 1.0 / math.sqrt(HD)
    whole = y_size > 1
    place.greet(REPLICAS if whole else 2)

    small_wide[...] = jnp.zeros_like(small_wide)
    for l in range(LAYERS):
        for k, ref in enumerate((gain1, shift1, out_bias, gain2, shift2, down_bias)):
            small_wide[6 * l + k : 6 * l + k + 1, :] = ref[l : l + 1, :].astype(F32)
        for k in range(2):
            small_wide[12 + 2 * l + k : 13 + 2 * l + k, :] = qv_bias[l : l + 1, k * OWN : (k + 1) * OWN].astype(F32)
        for k in range(4):
            small_wide[16 + 4 * l + k : 17 + 4 * l + k, :] = up_bias[l : l + 1, k * OWN : (k + 1) * OWN].astype(F32)
    small[...] = small_wide[...].astype(BF16)
    segs[...] = jnp.broadcast_to(own_ids[...], segs.shape)
    weights = Weights(links, place, (raw_qkv, raw_up, raw_out, raw_down), (w_qkv, w_up, w_out, w_down))
    small_sem, segs_sem = links.pair(), links.pair()
    for j in range(1, N):
        links.make(small, small_all.at[place.shard], place.at_shard(j), small_sem, small_sem).start()
    links.local(small, small_all.at[place.shard], small_sem)
    swap_tokens = Swap(links, place, tokens.at[0], token_in)
    weights.start(0, 0)
    here = place.core * N + place.shard
    for flip in range(2):
        for j in range(N):
            if flip + j > 0:
                links.make(segs, segs_all.at[here], place.at_block(flip, j), segs_sem, segs_sem).start()
    links.local(segs, segs_all.at[here], segs_sem)
    links.landed(small_all, small_sem)
    for s in range(N):
        vectors[:, s * OWN : (s + 1) * OWN] = small_all[s].astype(F32)
    swap_tokens.ready()
    state[0] = token_in[...].astype(F32)
    for head in range(2):
        power = (place.block * 2 + head + 1).astype(F32) * (-8.0 / H * math.log(2.0))
        slopes[head] = jnp.exp(jnp.full((1, QB), power, F32))
    outs = dict(zip(KINDS, (up_out, down_out, qkv_out, out_out)))
    parts = dict(zip(KINDS, (up_slots, down_slots, qkv_slots, out_slots)))
    totals = dict(zip(KINDS, (up_sum, down_sum, qkv_sum, out_sum)))
    sums = [None] * LAYERS
    for l in range(LAYERS):
        if whole:
            own_parts = {k: ref.at[l] for k, ref in parts.items()}
            own_totals = {k: ref.at[l] for k, ref in totals.items()}
            sums[l] = Sums(links, place, l, wide, tall, own_parts, own_totals, outs)
    smalls = SmallSums(links, place, mine, small_low, small_slots, small_sum, small_every, small_out)
    mine[...] = jnp.zeros_like(mine)

    def vector(l, k):
        return vectors[l * 6 + k : l * 6 + k + 1, :]

    def q_or_v_bias(l, base):
        cols = lanes_of(base + place.block // 2)
        even, odd = (vectors[12 + 2 * l + k : 13 + 2 * l + k, cols] for k in range(2))
        return jnp.where(place.block % 2 == 0, even, odd)

    def weight(ref, l, cols):
        return ref[l].reshape(D, cols)

    for l in range(LAYERS):
        rows_in = state[l]
        hidden1[l, own, :] = (standardize(rows_in)[0] * vector(l, 0) + vector(l, 1)).astype(BF16)
        if l == 0:
            weights.around(0, 0)
            landing = []

            def fetch(index, landing=landing):
                landing.append(index)
        bias = jnp.concatenate([q_or_v_bias(l, 0), jnp.zeros((1, OWN), F32), q_or_v_bias(l, 4)], axis=1)

        def project(index, l=l, bias=bias):
            rows = block(index)
            qkv[l, rows, :] = (dot(hidden1[l, rows, :], weight(w_qkv, l, WQ)) + bias).astype(BF16)

        if l == 0:
            gather(links, place, hidden1.at[l], fetch)
            weights.start_x()
            weights.start(1, 0)
            weights.start(0, 1)
            weights.start(1, 1)
            swap_cot = Swap(links, place, cotangent.at[0], cot_in)
            weights.ready(0, 0)
            for index in landing:
                project(index)
            links.landed(segs_all, segs_sem)
            for s in range(N):
                ids[:, s * OWN : (s + 1) * OWN] = segs_all[place.side * N + s].astype(F32)
            row = ids[0:1, :]
            start = jnp.zeros((1, GROUP), F32)
            for value in range(3):
                count = jnp.sum(jnp.where(row == value, 1.0, 0.0), axis=1, keepdims=True)
                start = start + jnp.where(row > value, count, 0.0)
            starts[...] = start.astype(jnp.int32)
        else:
            gather(links, place, hidden1.at[l], project)

        turned[...] = qkv[l, :, 2 * OWN : 3 * OWN].T

        def attend(head, carry, l=l):
            slope = slopes[head]
            own_v = pl.ds(pl.multiple_of(head * HD, HD), HD)
            for qb in range(GROUP // QB):
                cols = slice(qb * QB, (qb + 1) * QB)
                query = head_lanes(qkv[l, cols, 0:OWN], head) * jnp.asarray(factor, BF16)
                start = starts[:, cols]
                top = jnp.full((1, QB), MASKED, F32)
                chunks = (qb + 1) * QB // KC
                for c in range(chunks):
                    keys = slice(c * KC, (c + 1) * KC)
                    edge = (c + 1) * KC > qb * QB
                    s = masked_scores(qkv[l, keys, OWN : 2 * OWN], query, slope, start, c * KC, qb * QB, edge)
                    score_scr[keys, :] = s
                    top = jnp.maximum(top, jnp.max(s, axis=0, keepdims=True))
                total = jnp.zeros((1, QB), F32)
                acc = jnp.zeros((HD, QB), F32)
                for c in range(chunks):
                    keys = slice(c * KC, (c + 1) * KC)
                    e = jnp.exp(score_scr[keys, :] - top)
                    total = total + jnp.sum(e, axis=0, keepdims=True)
                    acc = acc + dot(turned[own_v, keys], e.astype(BF16))
                mixed_turned[own_v, cols] = acc / total
                lse[l, head, :, cols] = top + jnp.log(total)
            return carry

        if l == 0:
            weights.around(1, 0)
        lax.fori_loop(0, 2, attend, 0)
        mixed[l] = mixed_turned[...].T.astype(BF16)
        weights.ready_x(2, l)
        if l == 0:
            weights.around(0, 1)
            weights.around(1, 1)

        def out_part(index, l=l):
            return dot(mixed[l, block(index), :], w_out[l])

        middle[l] = state[l] + scatter(links, place, out_part, out_scr, slots) + vector(l, 2)
        hidden2[l, own, :] = (standardize(middle[l])[0] * vector(l, 3) + vector(l, 4)).astype(BF16)
        weights.ready(1, l)
        up_bias = jnp.concatenate([vectors[16 + 4 * l + k : 17 + 4 * l + k, lanes] for k in range(4)], axis=1)

        def up(index, l=l, up_bias=up_bias):
            rows = block(index)
            value, slope = gelu_pair(dot(hidden2[l, rows, :], weight(w_up, l, WU)) + up_bias)
            active[l, rows, :] = value.astype(BF16)
            act_slope[l, rows, :] = slope

        gather(links, place, hidden2.at[l], up)
        weights.ready_x(3, l)

        def down_part(index, l=l):
            return dot(active[l, block(index), :], w_down[l])

        result = middle[l] + scatter(links, place, down_part, out_scr, slots) + vector(l, 5)
        if l + 1 < LAYERS:
            state[l + 1] = result
            weights.ready(0, l + 1)
        else:
            low_out[...] = result.astype(BF16)
    swap_output = Swap(links, place, low_out, output.at[0])
    swap_cot.ready()
    grad[...] = cot_in[...].astype(F32)

    for l in reversed(range(LAYERS)):
        d_full[own, :] = grad[...].astype(BF16)

        def down_back(index, l=l):
            rows = block(index)
            d_upped[rows, :] = (dot(d_full[rows, :], w_down[l], NT) * act_slope[l, rows, :]).astype(BF16)

        gather(links, place, d_full, down_back)
        if whole and l + 1 < LAYERS:
            sums[l + 1].total("up", "down")

        def up_back(index, l=l):
            return dot(d_upped[block(index), :], weight(w_up, l, WU), NT)

        def down_grads(l=l):
            def step(i, carry):
                cols = lanes_of(i)
                tall[l, lanes_of(1 + i), :] = dot(active[l, :, cols], d_full[...], TN).astype(BF16)
                return carry

            lax.fori_loop(0, WU // OWN, step, 0)
            mine[16 * l + 5 : 16 * l + 6, lanes] = jnp.sum(d_full[:, lanes].astype(F32), axis=0, keepdims=True)

        def up_grads(l=l):
            def step(i, carry):
                cols = lanes_of(i)
                wide[l, cols, WQ:WA] = dot(hidden2[l, :, cols], d_upped[...], TN).astype(BF16)
                return carry

            lax.fori_loop(0, D // OWN, step, 0)
            total = jnp.sum(d_upped[...].astype(F32), axis=0, keepdims=True)
            for k in range(WU // OWN):
                mine[16 * l + 6 + k : 16 * l + 7 + k, lanes] = total[:, k * OWN : (k + 1) * OWN]
            if whole:
                sums[l].start("up", "down")

        d_hidden2 = scatter(links, place, up_back, out_scr, slots, (down_grads, up_grads))
        d_rows, d_gain, d_shift = normalize_back(middle[l], vector(l, 3), d_hidden2)
        mine[16 * l + 2 : 16 * l + 3, :] = d_gain
        mine[16 * l + 3 : 16 * l + 4, :] = d_shift
        grad[...] += d_rows
        branch[own, :] = grad[...].astype(BF16)

        def out_back(index, l=l):
            rows = block(index)
            d_mixed[rows, :] = dot(branch[rows, :], w_out[l], NT).astype(BF16)

        gather(links, place, branch, out_back)
        if whole and l + 1 < LAYERS:
            sums[l + 1].total("qkv", "out")
            sums[l + 1].share("up", "down")

        turned[...] = qkv[l, :, OWN : 2 * OWN].T
        dk_acc[...] = jnp.zeros_like(dk_acc)
        dv_acc[...] = jnp.zeros_like(dv_acc)

        def attend_back(head, carry, l=l):
            slope = slopes[head]
            own_k = pl.ds(pl.multiple_of(head * HD, HD), HD)
            for qb in range(GROUP // QB):
                cols = slice(qb * QB, (qb + 1) * QB)
                query = head_lanes(qkv[l, cols, 0:OWN], head) * jnp.asarray(factor, BF16)
                d_mix = head_lanes(d_mixed[cols, :], head)
                start = starts[:, cols]
                log_total = lse[l, head, :, cols]
                delta = jnp.zeros((1, QB), F32)
                chunks = (qb + 1) * QB // KC
                for c in range(chunks):
                    keys = slice(c * KC, (c + 1) * KC)
                    edge = (c + 1) * KC > qb * QB
                    s = masked_scores(qkv[l, keys, OWN : 2 * OWN], query, slope, start, c * KC, qb * QB, edge)
                    prob = jnp.exp(s - log_total)
                    d_prob = dot(qkv[l, keys, 2 * OWN : 3 * OWN], d_mix, NT)
                    delta = delta + jnp.sum(prob * d_prob, axis=0, keepdims=True)
                    score_scr[keys, :] = prob
                    dprob_scr[keys, :] = d_prob
                    dv_acc[keys, :] += dot(prob.astype(BF16), d_mix)
                acc = jnp.zeros((HD, QB), F32)
                for c in range(chunks):
                    keys = slice(c * KC, (c + 1) * KC)
                    d_score = (score_scr[keys, :] * (dprob_scr[keys, :] - delta)).astype(BF16)
                    dk_acc[keys, :] += dot(d_score, query)
                    acc = acc + dot(turned[own_k, keys], d_score)
                mixed_turned[own_k, cols] = acc * factor
            return carry

        lax.fori_loop(0, 2, attend_back, 0)
        d_qkv[:, 0:OWN] = mixed_turned[...].T.astype(BF16)
        d_qkv[:, OWN : 2 * OWN] = dk_acc[...].astype(BF16)
        d_qkv[:, 2 * OWN : 3 * OWN] = dv_acc[...].astype(BF16)

        def qkv_back(index, l=l):
            rows = block(index)
            w = weight(w_qkv, l, WQ)
            both = dot(d_qkv[rows, 0 : 2 * OWN], w[:, 0 : 2 * OWN], NT)
            return both + dot(d_qkv[rows, 2 * OWN : 3 * OWN], w[:, 2 * OWN : 3 * OWN], NT)

        def qkv_grads(l=l):
            def step(i, carry):
                cols = lanes_of(i)
                wide[l, cols, 0:WQ] = dot(hidden1[l, :, cols], d_qkv[...], TN).astype(BF16)
                return carry

            lax.fori_loop(0, D // OWN, step, 0)

        def out_grads(l=l):
            tall[l, 0:OWN, :] = dot(mixed[l], branch[...], TN).astype(BF16)
            if whole:
                sums[l].start("qkv", "out")
            mine[16 * l + 4 : 16 * l + 5, lanes] = jnp.sum(branch[:, lanes].astype(F32), axis=0, keepdims=True)
            total = jnp.sum(d_qkv[...].astype(F32), axis=0, keepdims=True)
            for first, base in ((0, 0), (2 * OWN, 4)):
                bias = total[:, first : first + OWN]
                cols = lanes_of(base + place.block // 2)
                for k in range(2):
                    mine[16 * l + 10 + k : 16 * l + 11 + k, cols] = jnp.where(place.block % 2 == k, bias, 0.0)

        d_hidden1 = scatter(links, place, qkv_back, out_scr, slots, (qkv_grads, out_grads))
        d_rows, d_gain, d_shift = normalize_back(state[l], vector(l, 0), d_hidden1)
        mine[16 * l + 0 : 16 * l + 1, :] = d_gain
        mine[16 * l + 1 : 16 * l + 2, :] = d_shift
        grad[...] += d_rows

    swap_grad = Swap(links, place, grad, tokens_grad.at[0])
    if whole:
        smalls.start()
        sums[1].share("qkv", "out")
        sums[0].total("up", "down")
        smalls.total()
        sums[0].total("qkv", "out")
        sums[0].share("up", "down")
        smalls.finish()
        sums[0].share("qkv", "out")
    else:
        up_out[...] = wide[...]
        down_out[...] = tall[...]
        small_out[...] = mine[...]
    swap_output.ready()
    swap_grad.ready()
    weights.finish()
    links.sent(small_all.at[0 : N - 1], small_sem)
    links.sent(segs_all.at[0 : 2 * N - 1], segs_sem)
    for swap in (swap_tokens, swap_cot, swap_output, swap_grad):
        swap.finish()
    if whole:
        for layer in sums:
            layer.finish()


def in_vmem(count):
    return [pl.BlockSpec(memory_space=pltpu.VMEM)] * count


def struct(shape, dtype):
    return jax.ShapeDtypeStruct(shape, dtype)


SMALL = 32


def run_blocks(y_size, *args):
    whole = y_size > 1
    shapes = part_shapes()
    if whole:
        grads = (
            struct((LAYERS, N, 2, HALF, WU), BF16),
            struct((LAYERS, WU, D), BF16),
            struct((LAYERS, N, 2, HALF, WQ), BF16),
            struct((LAYERS, OWN, D), BF16),
            struct((SMALL, OWN), F32),
        )
    else:
        empty = struct((8, OWN), F32)
        grads = (struct((LAYERS, D, WA), BF16), struct((LAYERS, OWN + WU, D), BF16), empty, empty, struct((SMALL, D), F32))
    outs = (struct((1, OWN, D), BF16), struct((1, OWN, D), F32)) + grads
    quarter = OWN // y_size
    v = pltpu.VMEM
    scratch = [v((LAYERS, D, WA), BF16), v((LAYERS, OWN + WU, D), BF16), v((SMALL, D), F32)]
    scratch += [v((LAYERS, PLANE - 1) + shapes[kind], BF16) for kind in KINDS]
    scratch += [v((LAYERS,) + shapes[kind], BF16) for kind in KINDS]
    scratch += [
        v((SMALL, D), BF16),
        v((N - 1, SMALL, OWN), BF16),
        v((SMALL, OWN), BF16),
        v((REPLICAS - 1, SMALL, OWN), BF16),
    ]
    scratch += [
        v((LAYERS, N, y_size, quarter, WQ), BF16),
        v((LAYERS, N, y_size, quarter, WU), BF16),
        v((LAYERS, OWN, D), BF16),
        v((LAYERS, WU, D), BF16),
        v((SMALL, OWN), F32),
        v((SMALL, OWN), BF16),
        v((8, OWN), jnp.int32),
        v((N, SMALL, OWN), BF16),
        v((2 * N, 8, OWN), jnp.int32),
        v((SMALL, D), F32),
        v((8, D), F32),
        v((1, D), jnp.int32),
        v((2, 1, QB), F32),
        v((OWN, D), BF16),
        v((OWN, D), BF16),
        v((LAYERS, OWN, D), F32),
        v((LAYERS, GROUP, D), BF16),
        v((LAYERS, GROUP, WQ), BF16),
        v((LAYERS, 2, 1, GROUP), F32),
        v((LAYERS, GROUP, OWN), BF16),
        v((LAYERS, OWN, D), F32),
        v((LAYERS, GROUP, D), BF16),
        v((LAYERS, GROUP, WU), F32),
        v((LAYERS, GROUP, WU), BF16),
        v((GROUP, QB), F32),
        v((GROUP, QB), F32),
        v((OWN, GROUP), BF16),
        v((OWN, GROUP), F32),
        v((GROUP, D), BF16),
        v((GROUP, WU), BF16),
        v((GROUP, D), BF16),
        v((GROUP, OWN), BF16),
        v((GROUP, WQ), BF16),
        v((GROUP, OWN), F32),
        v((GROUP, OWN), F32),
        v((7 * OWN, D), BF16),
        v((7 * OWN, D), BF16),
        v((OWN, D), BF16),
        v((OWN, D), F32),
    ]
    copies = 4 * LAYERS * (GATHER_COPIES + SCATTER_COPIES) + 64
    return pl.pallas_call(
        functools.partial(blocks_kernel, y_size),
        out_shape=outs,
        in_specs=in_vmem(2) + [pl.BlockSpec(memory_space=pl.ANY)] * 4 + in_vmem(9),
        out_specs=in_vmem(2) + [pl.BlockSpec(memory_space=pl.ANY if whole else pltpu.VMEM)] * 4 + in_vmem(1),
        scratch_shapes=scratch + [pltpu.SemaphoreType.DMA((copies,)), pltpu.SemaphoreType.DMA((copies,))],
        compiler_params=pltpu.CompilerParams(collective_id=1, has_side_effects=True, vmem_limit_bytes=VMEM_LIMIT),
        cost_estimate=pl.CostEstimate(flops=24 << 30, bytes_accessed=32 << 20, transcendentals=16 << 20),
    )(*args)


ROWS = 32


def unpack_kernel(up, down, qkv, out, small, up_grad, down_grad, qkv_grad, out_grad,
                  g_gain1, g_shift1, g_gain2, g_shift2, g_out_bias, g_down_bias, g_qv_bias, g_up_bias):
    for l in range(LAYERS):
        here = slice(l, l + 1)
        singles = (g_gain1, g_shift1, g_gain2, g_shift2, g_out_bias, g_down_bias)
        for k, ref in enumerate(singles):
            ref[here, :] = small[16 * l + k : 16 * l + k + 1, :]
        for k in range(4):
            g_up_bias[here, k * OWN : (k + 1) * OWN] = small[16 * l + 6 + k : 16 * l + 7 + k, :]
        for k in range(2):
            g_qv_bias[here, k * OWN : (k + 1) * OWN] = small[16 * l + 10 + k : 16 * l + 11 + k, :]
    for w in range(N):
        up_grad[0, :, w * WU : (w + 1) * WU] = up[0, w, 0].astype(F32)
        for part in range(3):
            cols = slice(part * D + w * OWN, part * D + (w + 1) * OWN)
            qkv_grad[0, :, cols] = qkv[0, w, 0, :, part * OWN : (part + 1) * OWN].astype(F32)
    down_grad[0] = down[0].astype(F32)
    out_grad[0] = out[0].astype(F32)


def unpack(up, down, qkv, out, small):
    steps = OWN // ROWS
    per_half = HALF // ROWS

    def pieces(width):
        return pl.BlockSpec((1, N, 1, ROWS, width), lambda l, i: (l, 0, i // per_half, i % per_half, 0))

    def plain(rows, width):
        return pl.BlockSpec((1, rows, width), lambda l, i: (l, i, 0))

    def fixed(rows, width):
        return pl.BlockSpec((rows, width), lambda l, i: (0, 0))

    narrow = [OWN] * 6 + [2 * OWN, WU]
    return pl.pallas_call(
        unpack_kernel,
        grid=(LAYERS, steps),
        in_specs=[pieces(WU), plain(WU // steps, D), pieces(WQ), plain(ROWS, D), fixed(SMALL, OWN)],
        out_specs=[plain(ROWS, FF), plain(WU // steps, D), plain(ROWS, 3 * D), plain(ROWS, D)]
        + [fixed(LAYERS, width) for width in narrow],
        out_shape=[
            struct((LAYERS, OWN, FF), F32),
            struct((LAYERS, WU, D), F32),
            struct((LAYERS, OWN, 3 * D), F32),
            struct((LAYERS, OWN, D), F32),
        ]
        + [struct((LAYERS, width), F32) for width in narrow],
        compiler_params=pltpu.CompilerParams(vmem_limit_bytes=VMEM_LIMIT),
    )(up, down, qkv, out, small)


def per_device(y_size, reduce, tokens, segment_ids, cotangent, gain1, shift1, qkv_weight, qv_bias, out_weight, out_bias,
               gain2, shift2, up_weight, up_bias, down_weight, down_bias):
    output, grad, up, down, qkv, out, small = run_blocks(
        y_size, tokens, cotangent, qkv_weight, up_weight, out_weight, down_weight,
        gain1, shift1, out_bias, gain2, shift2, down_bias, qv_bias, up_bias, segment_ids,
    )
    if reduce is not None:
        up, down, qkv, out, small = reduce(up, down, small)
    up, down, qkv, out, g1, s1, g2, s2, ob, db, qv, ub = unpack(up, down, qkv, out, small)
    return output, grad, g1, s1, qkv, qv, out, ob, g2, s2, up, ub, down, db


def solution(mesh, reduce=None):
    rows = P(None, "shard")
    tiles = P(None, "shard", None)
    tokens = P("replica", "shard", None)
    y_size = 4 if mesh.shape["replica"] == REPLICAS else 1
    return jax.shard_map(
        functools.partial(per_device, y_size, reduce),
        mesh=mesh,
        in_specs=(
            tokens, P("replica", "shard"), tokens,
            rows, rows, tiles, rows, tiles, rows, rows, rows, tiles, rows, tiles, rows,
        ),
        out_specs=(tokens, tokens, rows, rows, tiles, rows, tiles, rows, rows, rows, tiles, rows, tiles, rows),
        check_vma=False,
    )
```

time: 1810 us -> 347 us (0.19)
  waiting for transfers between devices: 1190 us -> 0 us
  Pallas kernels: 0 us -> 342 us
  blocking collectives: 336 us -> 0 us
  matrix products: 161 us -> 0 us
  local copies, waits for them, and re-layouts: 66 us -> 1.51 us
  other arithmetic: 31.3 us -> 0 us
    reduce_scatter x8 -> x0, waiting for transfers between devices: 595 us -> none  [the longest x2 188 us: share_grads(): lax.psum_scatter(g_down.astype(jnp.bfloat16), 'shard', scatter_dimension=...]
    all_gather x12 -> x0, waiting for transfers between devices: 475 us -> none  [the longest x2 176 us: per_device(): lax.all_gather(up_weight[index], 'shard', axis=0, tiled=True)]
    pallas_call x0 -> x2, Pallas kernels: none -> 342 us  [the longest x1 333 us: run_blocks(): pl.pallas_call(functools.partial(blocks_kernel, y_size), out_shape=outs,...]
    all_gather x17 -> x0, blocking collectives: 241 us -> none  [the longest x2 40.6 us: per_device(): lax.all_gather(up_bias[index], 'shard', axis=0, tiled=True)]
    dot_general x36 -> x0, matrix products: 161 us -> none  [the longest x2 15.1 us: backward_layer(): jnp.einsum('rd,fd->rf', d_down, w_down, preferred_element_type=jnp.float32)]
    unnamed x29 -> x0, waiting for transfers between devices: 95.2 us -> none
    psum x1 -> x0, blocking collectives: 68.6 us -> none  [share_grads(): lax.psum(o_gain_a.astype(jnp.bfloat16), 'replica').astype(jnp.float32)]
    unnamed x157 -> x6, local copies, waits for them, and re-layouts: 38 us -> 1.51 us
  transfers between devices with their start and end apart: 25 -> 0, of which waited for: 20 -> 0; matrix products, arithmetic and copies ran while one was open for 9% -> 0% of each run, Pallas kernels for 0% -> 0%
where the time goes in v1:
time: 347 us; the launch traced here: 344 us
  Pallas kernels  342 us (99%)
    pallas_call x1, Pallas kernels, run_blocks(): pl.pallas_call(functools.partial(blocks_kernel, y_size), out_shape=outs,...  333 us
    pallas_call x1, Pallas kernels, unpack(): pl.pallas_call(unpack_kernel, grid=(LAYERS, steps), in_specs=[pieces(WU),...  8.69 us

profile of v1, /device:TPU:5, one launch (start us, length us, event | category | flops | bytes accessed | tf_op | source)
XLA Modules:
  0.0 344.1 jit_solution(13942946081663322494)
XLA Ops:
  0.7 333.0 %shard_map.254 = (bf16[1,128,1024]{2,1,0:T(8,128)(2,1)}, f32[1,128,1024]{2,1,0:T(8,128)}, bf16[2,8,2,64,512]{4,3,2,1,0:T(8,128)(2,1)}, bf16[2,512,1024]{2,1,0:T(...) custom-call(bf16[1,128,1024]{2,1,0:T(8,128)(2,1)} %tokens.1, ...), custom_call_target="tpu_custom_call" | custom-call | flops 25769803776 | bytes 33554432 | tf_op jit(solution)/shard_map/pallas_call | solution.py:900
  333.6 0.0 copy-start.1
  333.6 0.0 copy-start
  333.6 8.7 %shard_map.255 = (f32[2,128,4096]{2,1,0:T(8,128)}, f32[2,512,1024]{2,1,0:T(8,128)}, f32[2,128,3072]{2,1,0:T(8,128)}, f32[2,128,1024]{2,1,0:T(8,128)}, f32[2,128]...) custom-call(bf16[2,8,2,64,512]{4,3,2,1,0:T(8,128)(2,1)} %get-tuple-e, ...), custom_call_target="tpu_custom_call" | custom-call | tf_op jit(solution)/shard_map/pallas_call | solution.py:948
  342.3 0.0 copy-done.1
  342.3 0.7 copy.31
  343.1 0.0 copy-done
  343.1 0.8 copy.32
Async XLA Ops:
  333.6 8.7 %copy-start.1 = (bf16[1,128,1024]{2,1,0:T(8,128)(2,1)S(1)}, bf16[1,128,1024]{2,1,0:T(8,128)(2,1)}, u32[]{:S(2)}) copy-start(bf16[1,128,1024]{2,1,0:T(8,128)(2,1)} %get-tuple-element.66) | copy-start | bytes 786436
  333.6 9.4 %copy-start = (f32[1,128,1024]{2,1,0:T(8,128)S(1)}, f32[1,128,1024]{2,1,0:T(8,128)}, u32[]{:S(2)}) copy-start(f32[1,128,1024]{2,1,0:T(8,128)} %get-tuple-element.67) | copy-start | bytes 1572868

commit v2 on v1

--- a/solution.py
+++ b/solution.py
@@ -70,13 +70,14 @@
         chip = self.chip - self.y + (self.y + j) % self.y_size
         return {"replica": chip * 2 + self.core}
 
-    def greet(self, replicas):
+    def greet(self, replicas, meanwhile):
         barrier = pltpu.get_barrier_semaphore()
         for i in range(N):
             for j in range(replicas):
                 if i + j > 0:
                     peer = {"shard": (self.shard + i) % N, "replica": (self.replica + j) % replicas}
                     pl.semaphore_signal(barrier, inc=1, device_id=peer, device_id_type=MESH)
+        meanwhile()
         pl.semaphore_wait(barrier, N * replicas - 1)
 
 
@@ -509,24 +510,26 @@
     lanes = lanes_of(place.block)
     factor = 1.0 / math.sqrt(HD)
     whole = y_size > 1
-    place.greet(REPLICAS if whole else 2)
-
-    small_wide[...] = jnp.zeros_like(small_wide)
-    for l in range(LAYERS):
-        for k, ref in enumerate((gain1, shift1, out_bias, gain2, shift2, down_bias)):
-            small_wide[6 * l + k : 6 * l + k + 1, :] = ref[l : l + 1, :].astype(F32)
-        for k in range(2):
-            small_wide[12 + 2 * l + k : 13 + 2 * l + k, :] = qv_bias[l : l + 1, k * OWN : (k + 1) * OWN].astype(F32)
-        for k in range(4):
-            small_wide[16 + 4 * l + k : 17 + 4 * l + k, :] = up_bias[l : l + 1, k * OWN : (k + 1) * OWN].astype(F32)
-    small[...] = small_wide[...].astype(BF16)
-    segs[...] = jnp.broadcast_to(own_ids[...], segs.shape)
+
+    def pack():
+        small_wide[...] = jnp.zeros_like(small_wide)
+        for l in range(LAYERS):
+            for k, ref in enumerate((gain1, shift1, out_bias, gain2, shift2, down_bias)):
+                small_wide[6 * l + k : 6 * l + k + 1, :] = ref[l : l + 1, :].astype(F32)
+            for k in range(2):
+                small_wide[12 + 2 * l + k : 13 + 2 * l + k, :] = qv_bias[l : l + 1, k * OWN : (k + 1) * OWN].astype(F32)
+            for k in range(4):
+                small_wide[16 + 4 * l + k : 17 + 4 * l + k, :] = up_bias[l : l + 1, k * OWN : (k + 1) * OWN].astype(F32)
+        small[...] = small_wide[...].astype(BF16)
+        segs[...] = jnp.broadcast_to(own_ids[...], segs.shape)
+
+    place.greet(REPLICAS if whole else 2, pack)
     weights = Weights(links, place, (raw_qkv, raw_up, raw_out, raw_down), (w_qkv, w_up, w_out, w_down))
     small_sem, segs_sem = links.pair(), links.pair()
+    swap_tokens = Swap(links, place, tokens.at[0], token_in)
     for j in range(1, N):
         links.make(small, small_all.at[place.shard], place.at_shard(j), small_sem, small_sem).start()
     links.local(small, small_all.at[place.shard], small_sem)
-    swap_tokens = Swap(links, place, tokens.at[0], token_in)
     weights.start(0, 0)
     here = place.core * N + place.shard
     for flip in range(2):
@@ -573,6 +576,11 @@
             landing = []
 
             def fetch(index, landing=landing):
+                if not landing:
+                    weights.start(1, 0)
+                    weights.start(0, 1)
+                    weights.start(1, 1)
+                    weights.start_x()
                 landing.append(index)
         bias = jnp.concatenate([q_or_v_bias(l, 0), jnp.zeros((1, OWN), F32), q_or_v_bias(l, 4)], axis=1)
 
@@ -582,10 +590,6 @@
 
         if l == 0:
             gather(links, place, hidden1.at[l], fetch)
-            weights.start_x()
-            weights.start(1, 0)
-            weights.start(0, 1)
-            weights.start(1, 1)
             swap_cot = Swap(links, place, cotangent.at[0], cot_in)
             weights.ready(0, 0)
             for index in landing:
@@ -690,6 +694,8 @@
                 return carry
 
             lax.fori_loop(0, WU // OWN, step, 0)
+            if whole:
+                sums[l].start("down")
             mine[16 * l + 5 : 16 * l + 6, lanes] = jnp.sum(d_full[:, lanes].astype(F32), axis=0, keepdims=True)
 
         def up_grads(l=l):
@@ -699,11 +705,11 @@
                 return carry
 
             lax.fori_loop(0, D // OWN, step, 0)
+            if whole:
+                sums[l].start("up")
             total = jnp.sum(d_upped[...].astype(F32), axis=0, keepdims=True)
             for k in range(WU // OWN):
                 mine[16 * l + 6 + k : 16 * l + 7 + k, lanes] = total[:, k * OWN : (k + 1) * OWN]
-            if whole:
-                sums[l].start("up", "down")
 
         d_hidden2 = scatter(links, place, up_back, out_scr, slots, (down_grads, up_grads))
         d_rows, d_gain, d_shift = normalize_back(middle[l], vector(l, 3), d_hidden2)
@@ -773,11 +779,13 @@
                 return carry
 
             lax.fori_loop(0, D // OWN, step, 0)
+            if whole:
+                sums[l].start("qkv")
 
         def out_grads(l=l):
             tall[l, 0:OWN, :] = dot(mixed[l], branch[...], TN).astype(BF16)
             if whole:
-                sums[l].start("qkv", "out")
+                sums[l].start("out")
             mine[16 * l + 4 : 16 * l + 5, lanes] = jnp.sum(branch[:, lanes].astype(F32), axis=0, keepdims=True)
             total = jnp.sum(d_qkv[...].astype(F32), axis=0, keepdims=True)
             for first, base in ((0, 0), (2 * OWN, 4)):

time: 347 us -> 316 us (0.911)
  Pallas kernels: 342 us -> 309 us
    pallas_call x1, Pallas kernels: 333 us -> 301 us  [run_blocks(): pl.pallas_call(functools.partial(blocks_kernel, y_size), out_shape=outs,...]
where the time goes in v2:
time: 316 us; the launch traced here: 312 us
  Pallas kernels  309 us (98%)
    pallas_call x1, Pallas kernels, run_blocks(): pl.pallas_call(functools.partial(blocks_kernel, y_size), out_shape=outs,...  301 us
    pallas_call x1, Pallas kernels, unpack(): pl.pallas_call(unpack_kernel, grid=(LAYERS, steps), in_specs=[pieces(WU),...  8.69 us

profile of v2, /device:TPU:5, one launch (start us, length us, event | category | flops | bytes accessed | tf_op | source)
XLA Modules:
  0.0 311.7 jit_solution(9289586807502676954)
XLA Ops:
  0.7 300.5 %shard_map.254 = (bf16[1,128,1024]{2,1,0:T(8,128)(2,1)}, f32[1,128,1024]{2,1,0:T(8,128)}, bf16[2,8,2,64,512]{4,3,2,1,0:T(8,128)(2,1)}, bf16[2,512,1024]{2,1,0:T(...) custom-call(bf16[1,128,1024]{2,1,0:T(8,128)(2,1)} %tokens.1, ...), custom_call_target="tpu_custom_call" | custom-call | flops 25769803776 | bytes 33554432 | tf_op jit(solution)/shard_map/pallas_call | solution.py:908
  301.2 0.0 copy-start.1
  301.2 0.0 copy-start
  301.2 8.7 %shard_map.255 = (f32[2,128,4096]{2,1,0:T(8,128)}, f32[2,512,1024]{2,1,0:T(8,128)}, f32[2,128,3072]{2,1,0:T(8,128)}, f32[2,128,1024]{2,1,0:T(8,128)}, f32[2,128]...) custom-call(bf16[2,8,2,64,512]{4,3,2,1,0:T(8,128)(2,1)} %get-tuple-e, ...), custom_call_target="tpu_custom_call" | custom-call | tf_op jit(solution)/shard_map/pallas_call | solution.py:956
  309.9 0.0 copy-done.1
  309.9 0.7 copy.31
  310.6 0.0 copy-done
  310.6 0.8 copy.32
Async XLA Ops:
  301.2 8.7 %copy-start.1 = (bf16[1,128,1024]{2,1,0:T(8,128)(2,1)S(1)}, bf16[1,128,1024]{2,1,0:T(8,128)(2,1)}, u32[]{:S(2)}) copy-start(bf16[1,128,1024]{2,1,0:T(8,128)(2,1)} %get-tuple-element.66) | copy-start | bytes 786436
  301.2 9.4 %copy-start = (f32[1,128,1024]{2,1,0:T(8,128)S(1)}, f32[1,128,1024]{2,1,0:T(8,128)}, u32[]{:S(2)}) copy-start(f32[1,128,1024]{2,1,0:T(8,128)} %get-tuple-element.67) | copy-start | bytes 1572868

commit v3 on v2

--- a/solution.py
+++ b/solution.py
@@ -362,63 +362,98 @@
 
 
 REPLICAS = 16
-PLANE = 16
 CHIPS = 8
 HALF = OWN // 2
 KINDS = ("up", "down", "qkv", "out")
 
 
 class Sums:
-    def __init__(self, links, place, l, wide, tall, slots, totals, outs):
+    def __init__(self, links, place, l, wide, tall, wholes, slots, totals, outs):
         self.links, self.p, self.l = links, place, l
         self.wide, self.tall = wide, tall
-        self.slots, self.totals, self.outs = slots, totals, outs
-        self.q = place.side * 8 + place.chip
+        self.wholes, self.slots, self.totals, self.outs = wholes, slots, totals, outs
+        self.along_x = place.side * 2 + place.chip // 4
+        self.along_y = place.chip % 4
+        self.around = links.pair(len(KINDS))
         self.sems = links.pair(len(KINDS))
         self.give = links.pair(len(KINDS))
         self.twin = links.pair(len(KINDS))
         self.last = {}
 
+    def first(self, kind):
+        return self.along_x if by_rows(kind) else self.along_y
+
+    def second(self, kind):
+        return self.along_y if by_rows(kind) else self.along_x
+
+    def number(self, kind):
+        return self.first(kind) * 4 + self.second(kind)
+
+    def at(self, x, y):
+        return {"shard": (x // 2) * 4 + self.p.z, "replica": ((x % 2) * 4 + y) * 2 + self.p.core}
+
+    def group(self, kind, first):
+        if by_rows(kind):
+            cols = slice(WQ, WA) if kind == "up" else slice(0, WQ)
+            return self.wide.at[self.l, block_of(first, 4 * HALF), cols]
+        rows = WU // 4 if kind == "down" else OWN // 4
+        start = OWN if kind == "down" else 0
+        return self.tall.at[self.l, pl.ds(pl.multiple_of(start + first * rows, 16), rows), :]
+
     def part(self, kind, q):
-        if kind == "up":
-            return self.wide.at[self.l, block_of(q, HALF), WQ:WA]
-        if kind == "qkv":
-            return self.wide.at[self.l, block_of(q, HALF), 0:WQ]
+        if by_rows(kind):
+            cols = slice(WQ, WA) if kind == "up" else slice(0, WQ)
+            return self.wide.at[self.l, block_of(q, HALF), cols]
         rows = WU // 8 if kind == "down" else OWN // 8
-        first = OWN if kind == "down" else 0
-        return self.tall.at[self.l, pl.ds(pl.multiple_of(first + (q // 2) * rows, 16), rows), half_of(q % 2)]
+        start = OWN if kind == "down" else 0
+        return self.tall.at[self.l, pl.ds(pl.multiple_of(start + (q // 2) * rows, 16), rows), half_of(q % 2)]
 
     def target(self, kind):
-        out = self.outs[kind]
-        if kind in ("up", "qkv"):
-            return out.at[self.l, self.p.block, self.q % 2]
+        out, q = self.outs[kind], self.number(kind)
+        if by_rows(kind):
+            return out.at[self.l, self.p.block, q % 2]
         rows = WU // 8 if kind == "down" else OWN // 8
-        return out.at[self.l, block_of(self.q // 2, rows), half_of(self.q % 2)]
+        return out.at[self.l, block_of(q // 2, rows), half_of(q % 2)]
 
     def region(self, kind, core):
         out = self.outs[kind]
-        return out.at[self.l, pl.ds(core * 4, 4)] if kind in ("up", "qkv") else out.at[self.l, :, half_of(core)]
+        return out.at[self.l, pl.ds(core * 4, 4)] if by_rows(kind) else out.at[self.l, :, half_of(core)]
 
     def start(self, *kinds):
         for kind in kinds:
+            sem = self.around + KINDS.index(kind)
+            for j in range(1, 4):
+                other = (self.first(kind) + j) % 4
+                peer = self.at(other, self.along_y) if by_rows(kind) else self.at(self.along_x, other)
+                self.links.make(self.group(kind, other), self.wholes[kind].at[j - 1], peer, sem, sem).start()
+
+    def middle(self, *kinds):
+        for kind in kinds:
+            wholes = self.wholes[kind]
+            self.links.landed(wholes, self.around + KINDS.index(kind))
+            group = self.group(kind, self.first(kind))
+            total = group[...].astype(F32)
+            for j in range(3):
+                total = total + wholes[j].astype(F32)
+            group[...] = total.astype(BF16)
             sem = self.sems + KINDS.index(kind)
-            for j in range(1, PLANE):
-                q = (self.q + j) % PLANE
-                peer = {"shard": (q // 8) * 4 + self.p.z, "replica": (q % 8) * 2 + self.p.core}
-                self.links.make(self.part(kind, q), self.slots[kind].at[j - 1], peer, sem, sem).start()
+            for j in range(1, 4):
+                other = (self.second(kind) + j) % 4
+                peer = self.at(self.along_x, other) if by_rows(kind) else self.at(other, self.along_y)
+                part = self.part(kind, self.first(kind) * 4 + other)
+                self.links.make(part, self.slots[kind].at[j - 1], peer, sem, sem).start()
 
     def total(self, *kinds):
         for kind in kinds:
-            slots = self.slots[kind]
+            slots, q = self.slots[kind], self.number(kind)
             self.links.landed(slots, self.sems + KINDS.index(kind))
-            part = self.part(kind, self.q)[...].astype(F32)
-            for j in range(PLANE - 1):
+            part = self.part(kind, q)[...].astype(F32)
+            for j in range(3):
                 part = part + slots[j].astype(F32)
             self.totals[kind][...] = part.astype(BF16)
             sem = self.give + KINDS.index(kind)
-            by_rows = kind in ("up", "qkv")
-            shard = self.q // 2 if by_rows else self.p.block
-            core = self.p.core if by_rows else self.q % 2
+            shard = q // 2 if by_rows(kind) else self.p.block
+            core = self.p.core if by_rows(kind) else q % 2
             target = self.target(kind)
             for j in range(1, CHIPS):
                 peer = {"shard": shard, "replica": ((self.p.chip + j) % CHIPS) * 2 + core}
@@ -441,18 +476,30 @@
             region = self.region(kind, self.p.core)
             self.links.landed(region, self.twin + index)
             self.links.sent(region, self.twin + index)
+            self.links.sent(self.wholes[kind], self.around + index)
             self.links.sent(self.slots[kind], self.sems + index)
-            self.links.sent(self.slots[kind].at[0 : CHIPS - 1], self.give + index)
+            out = self.outs[kind]
+            rows = (CHIPS - 1) * self.totals[kind].shape[0]
+            given = out.at[self.l, 0 : CHIPS - 1, 0] if by_rows(kind) else out.at[self.l, 0:rows, 0 : D // 2]
+            self.links.sent(given, self.give + index)
             mine, last = self.last[kind]
             pl.when(jnp.logical_not(mine))(last.wait_send)
 
 
+def by_rows(kind):
+    return kind in ("up", "qkv")
+
+
 def block_of(index, rows):
     return pl.ds(pl.multiple_of(index * rows, 16), rows)
 
 
 def half_of(index):
     return pl.ds(pl.multiple_of(index * (D // 2), OWN), D // 2)
+
+
+def group_shapes():
+    return {"up": (4 * HALF, WU), "down": (WU // 4, D), "qkv": (4 * HALF, WQ), "out": (OWN // 4, D)}
 
 
 def part_shapes():
@@ -497,7 +544,7 @@
     tokens, cotangent, raw_qkv, raw_up, raw_out, raw_down, gain1, shift1, out_bias, gain2, shift2, down_bias,
     qv_bias, up_bias, own_ids,
     output, tokens_grad, up_out, down_out, qkv_out, out_out, small_out,
-    wide, tall, mine, up_slots, down_slots, qkv_slots, out_slots, up_sum, down_sum, qkv_sum, out_sum,
+    wide, tall, mine, up_groups, down_groups, qkv_groups, out_groups, up_slots, down_slots, qkv_slots, out_slots, up_sum, down_sum, qkv_sum, out_sum,
     small_low, small_slots, small_sum, small_every,
     w_qkv, w_up, w_out, w_down, small_wide, small, segs, small_all, segs_all, vectors, ids, starts, slopes,
     token_in, cot_in, state, hidden1, qkv, lse, mixed, middle, hidden2, act_slope, active,
@@ -547,13 +594,15 @@
         slopes[head] = jnp.exp(jnp.full((1, QB), power, F32))
     outs = dict(zip(KINDS, (up_out, down_out, qkv_out, out_out)))
     parts = dict(zip(KINDS, (up_slots, down_slots, qkv_slots, out_slots)))
+    groups = dict(zip(KINDS, (up_groups, down_groups, qkv_groups, out_groups)))
     totals = dict(zip(KINDS, (up_sum, down_sum, qkv_sum, out_sum)))
     sums = [None] * LAYERS
     for l in range(LAYERS):
         if whole:
             own_parts = {k: ref.at[l] for k, ref in parts.items()}
+            own_groups = {k: ref.at[l] for k, ref in groups.items()}
             own_totals = {k: ref.at[l] for k, ref in totals.items()}
-            sums[l] = Sums(links, place, l, wide, tall, own_parts, own_totals, outs)
+            sums[l] = Sums(links, place, l, wide, tall, own_groups, own_parts, own_totals, outs)
     smalls = SmallSums(links, place, mine, small_low, small_slots, small_sum, small_every, small_out)
     mine[...] = jnp.zeros_like(mine)
 
@@ -682,7 +731,8 @@
 
         gather(links, place, d_full, down_back)
         if whole and l + 1 < LAYERS:
-            sums[l + 1].total("up", "down")
+            sums[l + 1].total("down", "up")
+            sums[l + 1].middle("out", "qkv")
 
         def up_back(index, l=l):
             return dot(d_upped[block(index), :], weight(w_up, l, WU), NT)
@@ -724,8 +774,8 @@
 
         gather(links, place, branch, out_back)
         if whole and l + 1 < LAYERS:
-            sums[l + 1].total("qkv", "out")
-            sums[l + 1].share("up", "down")
+            sums[l + 1].total("out", "qkv")
+            sums[l + 1].share("down", "up")
 
         turned[...] = qkv[l, :, OWN : 2 * OWN].T
         dk_acc[...] = jnp.zeros_like(dk_acc)
@@ -762,6 +812,10 @@
             return carry
 
         lax.fori_loop(0, 2, attend_back, 0)
+        if whole:
+            sums[l].middle("down", "up")
+            if l + 1 < LAYERS:
+                sums[l + 1].share("out", "qkv")
         d_qkv[:, 0:OWN] = mixed_turned[...].T.astype(BF16)
         d_qkv[:, OWN : 2 * OWN] = dk_acc[...].astype(BF16)
         d_qkv[:, 2 * OWN : 3 * OWN] = dv_acc[...].astype(BF16)
@@ -786,6 +840,8 @@
             tall[l, 0:OWN, :] = dot(mixed[l], branch[...], TN).astype(BF16)
             if whole:
                 sums[l].start("out")
+                if l == 0:
+                    sums[l].total("down", "up")
             mine[16 * l + 4 : 16 * l + 5, lanes] = jnp.sum(branch[:, lanes].astype(F32), axis=0, keepdims=True)
             total = jnp.sum(d_qkv[...].astype(F32), axis=0, keepdims=True)
             for first, base in ((0, 0), (2 * OWN, 4)):
@@ -803,13 +859,12 @@
     swap_grad = Swap(links, place, grad, tokens_grad.at[0])
     if whole:
         smalls.start()
-        sums[1].share("qkv", "out")
-        sums[0].total("up", "down")
+        sums[0].middle("out", "qkv")
         smalls.total()
-        sums[0].total("qkv", "out")
-        sums[0].share("up", "down")
+        sums[0].total("out", "qkv")
+        sums[0].share("down", "up")
         smalls.finish()
-        sums[0].share("qkv", "out")
+        sums[0].share("out", "qkv")
     else:
         up_out[...] = wide[...]
         down_out[...] = tall[...]
@@ -855,7 +910,8 @@
     quarter = OWN // y_size
     v = pltpu.VMEM
     scratch = [v((LAYERS, D, WA), BF16), v((LAYERS, OWN + WU, D), BF16), v((SMALL, D), F32)]
-    scratch += [v((LAYERS, PLANE - 1) + shapes[kind], BF16) for kind in KINDS]
+    scratch += [v((LAYERS, 3) + group_shapes()[kind], BF16) for kind in KINDS]
+    scratch += [v((LAYERS, 3) + shapes[kind], BF16) for kind in KINDS]
     scratch += [v((LAYERS,) + shapes[kind], BF16) for kind in KINDS]
     scratch += [
         v((SMALL, D), BF16),

time: 316 us -> 320 us (1.013)
  Pallas kernels: 309 us -> 314 us
    pallas_call x1, Pallas kernels: 301 us -> 305 us  [run_blocks(): pl.pallas_call(functools.partial(blocks_kernel, y_size), out_shape=outs,...]
where the time goes in v3:
time: 320 us; the launch traced here: 317 us
  Pallas kernels  314 us (98%)
    pallas_call x1, Pallas kernels, run_blocks(): pl.pallas_call(functools.partial(blocks_kernel, y_size), out_shape=outs,...  305 us
    pallas_call x1, Pallas kernels, unpack(): pl.pallas_call(unpack_kernel, grid=(LAYERS, steps), in_specs=[pieces(WU),...  8.69 us

profile of v3, /device:TPU:5, one launch (start us, length us, event | category | flops | bytes accessed | tf_op | source)
XLA Modules:
  0.0 316.6 jit_solution(1054031328243073890)
XLA Ops:
  0.7 305.5 %shard_map.254 = (bf16[1,128,1024]{2,1,0:T(8,128)(2,1)}, f32[1,128,1024]{2,1,0:T(8,128)}, bf16[2,8,2,64,512]{4,3,2,1,0:T(8,128)(2,1)}, bf16[2,512,1024]{2,1,0:T(...) custom-call(bf16[1,128,1024]{2,1,0:T(8,128)(2,1)} %tokens.1, ...), custom_call_target="tpu_custom_call" | custom-call | flops 25769803776 | bytes 33554432 | tf_op jit(solution)/shard_map/pallas_call | solution.py:964
  306.1 0.0 copy-start.1
  306.1 0.0 copy-start
  306.1 8.7 %shard_map.255 = (f32[2,128,4096]{2,1,0:T(8,128)}, f32[2,512,1024]{2,1,0:T(8,128)}, f32[2,128,3072]{2,1,0:T(8,128)}, f32[2,128,1024]{2,1,0:T(8,128)}, f32[2,128]...) custom-call(bf16[2,8,2,64,512]{4,3,2,1,0:T(8,128)(2,1)} %get-tuple-e, ...), custom_call_target="tpu_custom_call" | custom-call | tf_op jit(solution)/shard_map/pallas_call | solution.py:1012
  314.8 0.0 copy-done.1
  314.9 0.7 copy.31
  315.6 0.0 copy-done
  315.6 0.8 copy.32
Async XLA Ops:
  306.1 8.7 %copy-start.1 = (bf16[1,128,1024]{2,1,0:T(8,128)(2,1)S(1)}, bf16[1,128,1024]{2,1,0:T(8,128)(2,1)}, u32[]{:S(2)}) copy-start(bf16[1,128,1024]{2,1,0:T(8,128)(2,1)} %get-tuple-element.66) | copy-start | bytes 786436
  306.1 9.4 %copy-start = (f32[1,128,1024]{2,1,0:T(8,128)S(1)}, f32[1,128,1024]{2,1,0:T(8,128)}, u32[]{:S(2)}) copy-start(f32[1,128,1024]{2,1,0:T(8,128)} %get-tuple-element.67) | copy-start | bytes 1572868

commit v4 on v3

--- a/solution.py
+++ b/solution.py
@@ -621,11 +621,11 @@
         rows_in = state[l]
         hidden1[l, own, :] = (standardize(rows_in)[0] * vector(l, 0) + vector(l, 1)).astype(BF16)
         if l == 0:
-            weights.around(0, 0)
             landing = []
 
             def fetch(index, landing=landing):
                 if not landing:
+                    weights.around(0, 0)
                     weights.start(1, 0)
                     weights.start(0, 1)
                     weights.start(1, 1)
@@ -730,9 +730,6 @@
             d_upped[rows, :] = (dot(d_full[rows, :], w_down[l], NT) * act_slope[l, rows, :]).astype(BF16)
 
         gather(links, place, d_full, down_back)
-        if whole and l + 1 < LAYERS:
-            sums[l + 1].total("down", "up")
-            sums[l + 1].middle("out", "qkv")
 
         def up_back(index, l=l):
             return dot(d_upped[block(index), :], weight(w_up, l, WU), NT)
@@ -757,6 +754,9 @@
             lax.fori_loop(0, D // OWN, step, 0)
             if whole:
                 sums[l].start("up")
+                if l + 1 < LAYERS:
+                    sums[l + 1].total("down", "up")
+                    sums[l + 1].middle("out", "qkv")
             total = jnp.sum(d_upped[...].astype(F32), axis=0, keepdims=True)
             for k in range(WU // OWN):
                 mine[16 * l + 6 + k : 16 * l + 7 + k, lanes] = total[:, k * OWN : (k + 1) * OWN]
@@ -812,10 +812,6 @@
             return carry
 
         lax.fori_loop(0, 2, attend_back, 0)
-        if whole:
-            sums[l].middle("down", "up")
-            if l + 1 < LAYERS:
-                sums[l + 1].share("out", "qkv")
         d_qkv[:, 0:OWN] = mixed_turned[...].T.astype(BF16)
         d_qkv[:, OWN : 2 * OWN] = dk_acc[...].astype(BF16)
         d_qkv[:, 2 * OWN : 3 * OWN] = dv_acc[...].astype(BF16)
@@ -835,13 +831,14 @@
             lax.fori_loop(0, D // OWN, step, 0)
             if whole:
                 sums[l].start("qkv")
+                sums[l].middle("down", "up")
 
         def out_grads(l=l):
             tall[l, 0:OWN, :] = dot(mixed[l], branch[...], TN).astype(BF16)
             if whole:
                 sums[l].start("out")
-                if l == 0:
-                    sums[l].total("down", "up")
+                if l + 1 < LAYERS:
+                    sums[l + 1].share("out", "qkv")
             mine[16 * l + 4 : 16 * l + 5, lanes] = jnp.sum(branch[:, lanes].astype(F32), axis=0, keepdims=True)
             total = jnp.sum(d_qkv[...].astype(F32), axis=0, keepdims=True)
             for first, base in ((0, 0), (2 * OWN, 4)):
@@ -859,6 +856,7 @@
     swap_grad = Swap(links, place, grad, tokens_grad.at[0])
     if whole:
         smalls.start()
+        sums[0].total("down", "up")
         sums[0].middle("out", "qkv")
         smalls.total()
         sums[0].total("out", "qkv")

time: 320 us -> 322 us (level)
  no operation moved by 1% of the time
where the time goes in v4:
time: 322 us; the launch traced here: 318 us
  Pallas kernels  315 us (98%)
    pallas_call x1, Pallas kernels, run_blocks(): pl.pallas_call(functools.partial(blocks_kernel, y_size), out_shape=outs,...  306 us
    pallas_call x1, Pallas kernels, unpack(): pl.pallas_call(unpack_kernel, grid=(LAYERS, steps), in_specs=[pieces(WU),...  8.69 us

profile of v4, /device:TPU:5, one launch (start us, length us, event | category | flops | bytes accessed | tf_op | source)
XLA Modules:
  0.0 317.6 jit_solution(2278822409865981250)
XLA Ops:
  0.7 306.5 %shard_map.254 = (bf16[1,128,1024]{2,1,0:T(8,128)(2,1)}, f32[1,128,1024]{2,1,0:T(8,128)}, bf16[2,8,2,64,512]{4,3,2,1,0:T(8,128)(2,1)}, bf16[2,512,1024]{2,1,0:T(...) custom-call(bf16[1,128,1024]{2,1,0:T(8,128)(2,1)} %tokens.1, ...), custom_call_target="tpu_custom_call" | custom-call | flops 25769803776 | bytes 33554432 | tf_op jit(solution)/shard_map/pallas_call | solution.py:962
  307.1 0.0 copy-start.1
  307.1 0.0 copy-start
  307.1 8.7 %shard_map.255 = (f32[2,128,4096]{2,1,0:T(8,128)}, f32[2,512,1024]{2,1,0:T(8,128)}, f32[2,128,3072]{2,1,0:T(8,128)}, f32[2,128,1024]{2,1,0:T(8,128)}, f32[2,128]...) custom-call(bf16[2,8,2,64,512]{4,3,2,1,0:T(8,128)(2,1)} %get-tuple-e, ...), custom_call_target="tpu_custom_call" | custom-call | tf_op jit(solution)/shard_map/pallas_call | solution.py:1010
  315.8 0.0 copy-done.1
  315.8 0.7 copy.31
  316.5 0.0 copy-done
  316.5 0.8 copy.32
Async XLA Ops:
  307.1 8.7 %copy-start.1 = (bf16[1,128,1024]{2,1,0:T(8,128)(2,1)S(1)}, bf16[1,128,1024]{2,1,0:T(8,128)(2,1)}, u32[]{:S(2)}) copy-start(bf16[1,128,1024]{2,1,0:T(8,128)(2,1)} %get-tuple-element.66) | copy-start | bytes 786436
  307.1 9.4 %copy-start = (f32[1,128,1024]{2,1,0:T(8,128)S(1)}, f32[1,128,1024]{2,1,0:T(8,128)}, u32[]{:S(2)}) copy-start(f32[1,128,1024]{2,1,0:T(8,128)} %get-tuple-element.67) | copy-start | bytes 1572868
